TPU v7x, 128 devices: a whole 4x4x4 slice. The times are simulated.
128 devices in a mesh: fib: 16 (over y, x), row: 4 (over z), slab: 2 (over core).
Axes of the slice: x: 4, y: 4, z: 4, core: 2. Of those that a mesh axis runs over, the one named last changes fastest.
Arguments:
- tensor: float32 [512, 128, 64, 128], P('fib', 'row', 'slab'), may hold values from -300 to 300
- factor_one: float32 [512, 64], replicated, may hold values from -0.25 to 0.25
- factor_two: float32 [128, 64], P('row'), may hold values from -50 to 50
- factor_three: float32 [64, 64], P('slab'), may hold values from -50 to 50
- factor_four: float32 [128, 64], replicated, may hold values from -0.5 to 0.5
Outputs:
- updated_factor: float32 [512, 64], replicated
- core_tensor: float32 [64, 64, 64, 64], P(None, ('row', 'slab'), 'fib')
All inputs are finite; a program needn't handle non-finite values.
Results may differ from a plain program's by a relative error of at most 0.00015.
Values sent between devices are 32-bit elements; how exact they have to be, the bound alone decides.
A program may use at most 256 MiB of HBM per device.

v0:
```python
import jax
import jax.numpy as jnp
from jax import lax
from jax.sharding import PartitionSpec as P


def orthonormal(target):
    highest = lax.Precision.HIGHEST
    result = target
    for repeat in range(2):
        crossed = jnp.dot(result.T, result, precision=highest)
        cholesky_factor = jnp.linalg.cholesky(crossed)
        result = jax.scipy.linalg.solve_triangular(cholesky_factor, result.T, lower=True).T
    return result


def body(tensor, factor_one, factor_two, factor_three, factor_four):
    highest = lax.Precision.HIGHEST
    reduced = jnp.einsum("ijkl,lr->ijkr", tensor, factor_four, precision=highest)
    halfway = jnp.einsum("ijkr,jq->qikr", reduced, factor_two, precision=highest)
    summed = lax.psum_scatter(
        jnp.einsum("qikr,kp->qipr", halfway, factor_three, precision=highest),
        ("row", "slab"),
        scatter_dimension=0,
        tiled=True,
    )
    fibers = lax.all_to_all(summed, "fib", split_axis=2, concat_axis=1, tiled=True)
    local_gram = jnp.einsum("qipr,qjpr->ij", fibers, fibers, precision=highest)
    gram = lax.psum(local_gram, ("fib", "row", "slab"))
    target = jnp.dot(gram, factor_one, precision=highest)
    updated = orthonormal(target)
    core = jnp.einsum("ia,qipr->aqpr", updated, fibers, precision=highest)
    return (updated, core)


def solution(mesh):
    in_specs = (P("fib", "row", "slab", None), P(), P("row", None), P("slab", None), P())
    out_specs = (P(), P(None, ("row", "slab"), "fib", None))
    return jax.shard_map(body, mesh=mesh, in_specs=in_specs, out_specs=out_specs, check_vma=False)
```

profile of v0, /device:TPU:1, one launch (start us, length us, event | category | flops | bytes accessed | tf_op | source)
XLA Modules:
  0.0 893.4 jit_solution(1164375106009777697)
XLA Ops:
  7.2 26.5 %fusion = f32[32,32,32,64]{3,1,2,0:T(8,128)S(1)} fusion(f32[32,32,32,128]{3,2,1,0:T(8,128)} %param.8, f32[128,64]{0,1:T(8,128)} %param.12), kind=kOutput, calls=%fused_computation.1 | convolution fusion | flops 3221225472 | bytes 25198592 | tf_op jit(solution)/shard_map/ijkl,lr->ijkr/dot_general | solution.py:19
  33.7 56.3 %convolution_bitcast_fusion.1 = f32[64,32,32,64]{0,3,2,1:T(8,128)} fusion(f32[32,32,32,64]{3,1,2,0:T(8,128)S(1)} %fusion, f32[32,64]{1,0:T(8,128)S(1)} %copy-done.3), kind=kOutput, calls=%fused_computation.3 | convolution fusion | flops 1610612736 | bytes 25174016 | tf_op jit(solution)/shard_map/ijkr,jq->qikr/dot_general | solution.py:20
  90.0 34.8 %copy.18 = f32[64,32,32,64]{3,2,1,0:T(8,128)} copy(f32[64,32,32,64]{0,3,2,1:T(8,128)} %convolution_bitcast_fusion.1) | data formatting | bytes 33554432 | tf_op jit(solution)/shard_map/ijkr,jq->qikr/dot_general | solution.py:20
  124.8 111.6 %convolution_bitcast_fusion = f32[64,32,64,64]{2,3,1,0:T(8,128)} fusion(f32[64,32,32,64]{3,2,1,0:T(8,128)} %copy.18, f32[32,64]{1,0:T(8,128)S(1)} %copy-done.4), kind=kOutput, calls=%fused_computation | convolution fusion | flops 3221225472 | bytes 50339840 | tf_op jit(solution)/shard_map/qikr,kp->qipr/dot_general | solution.py:22
  236.6 330.5 %reduce-scatter.2.cloned.1.call-done = f32[8,32,64,64]{2,3,1,0:T(8,128)} async-done(((f32[64,32,64,64]{2,3,1,0:T(8,128)}), f32[8,32,64,64]{2,3,1,0:T(8,128)}) %reduce-scatter.2.cloned.1.call-update) | async-done | bytes 4194320 | tf_op jit(solution)/shard_map/reduce_scatter | solution.py:21
  567.1 9.6 %copy.19 = f32[8,32,64,64]{3,1,0,2:T(8,128)} copy(f32[8,32,64,64]{2,3,1,0:T(8,128)} %reduce-scatter.2.cloned.1.call-done) | data formatting | bytes 8388608 | tf_op jit(solution)/shard_map/reduce_scatter | solution.py:21
  576.7 13.3 %reshape.17 = f32[16,1,65536]{2,1,0:T(1,128)} reshape(f32[64,8,32,64]{3,2,1,0:T(8,128)} %bitcast.68) | data formatting | bytes 8388608
  589.9 56.4 %all_to_all.18 = f32[16,1,65536]{2,1,0:T(1,128)} all-to-all(f32[16,1,65536]{2,1,0:T(1,128)} %reshape.17), channel_id=1, replica_groups=mesh['fib'=16,'row'=4,'slab'=2] {'fib'}, dimensions={0} | all-to-all | bytes 8388608 | tf_op jit(solution)/shard_map/all_to_all | solution.py:27
  646.3 0.5 broadcast.36
  646.8 13.7 %reduce.4 = f32[16,65536]{1,0:T(8,128)} reduce(f32[16,1,65536]{2,1,0:T(1,128)} %all_to_all.18, f32[]{:T(128)} %broadcast.36), dimensions={1}, to_apply=%all_to_all.13.reduce_sub_computation | reduce | bytes 8388612 | tf_op jit(solution)/shard_map/all_to_all | solution.py:27
  660.6 6.9 reshape.18
  667.5 4.4 copy.21
  671.9 3.2 copy-done.1
  675.1 27.0 %fusion.4 = f32[512,512]{1,0:T(8,128)} fusion(f32[8,512,4,64]{3,1,2,0:T(8,128)S(1)} %bitcast.66), kind=kOutput, calls=%fused_computation.6 | convolution fusion | flops 6442450944 | bytes 5242880 | tf_op jit(solution)/shard_map/qipr,qjpr->ij/dot_general | solution.py:28
  702.1 147.0 %all-reduce.2.cloned.1.call-done = f32[512,512]{1,0:T(8,128)} async-done(((f32[512,512]{1,0:T(8,128)}), f32[512,512]{1,0:T(8,128)}) %all-reduce.2.cloned.1.call-update) | async-done | bytes 1048592 | tf_op jit(solution)/shard_map/psum | solution.py:29
  849.2 2.4 fusion.23
  851.5 0.3 fusion.24
  851.8 0.1 copy.24
  851.9 5.8 cholesky.44
  857.8 0.6 compare_reduce_fusion.1
  858.4 0.7 fusion.11
  859.1 4.9 custom-call.6
  864.0 0.3 fusion.9
  864.3 0.3 fusion.25
  864.6 0.1 copy.25
  864.7 5.8 cholesky.55
  870.5 0.6 compare_reduce_fusion
  871.2 0.7 fusion.12
  871.8 4.9 custom-call.7
  876.7 0.3 fusion.14
  877.1 7.5 fusion.7
  884.6 1.6 copy.27
  (17 shorter events, 0.2 us)
Async XLA Ops:
  7.2 842.0 %copy-start = (f32[512,64]{0,1:T(8,128)S(1)}, f32[512,64]{0,1:T(8,128)}, u32[]{:S(2)}) copy-start(f32[512,64]{0,1:T(8,128)} %param.9) | copy-start | bytes 393220
  7.2 26.6 %copy-start.3 = (f32[32,64]{1,0:T(8,128)S(1)}, f32[32,64]{1,0:T(8,128)}, u32[]{:S(2)}) copy-start(f32[32,64]{1,0:T(8,128)} %param.10) | copy-start | bytes 24580
  7.2 559.9 %reduce-scatter.2.cloned.1.call-start = ((), (), s32[]{:S(2)}) async-start(), calls=%async_computation.2 | async-start | bytes 75497472 | tf_op jit(solution)/shard_map/reduce_scatter | solution.py:21
  90.0 34.8 %copy-start.4 = (f32[32,64]{1,0:T(8,128)S(1)}, f32[32,64]{1,0:T(8,128)}, u32[]{:S(2)}) copy-start(f32[32,64]{1,0:T(8,128)} %param.11) | copy-start | bytes 24580
  236.5 612.7 %all-reduce.2.cloned.1.call-start = ((), (), s32[]{:S(2)}) async-start(), calls=%async_computation.3 | async-start | bytes 2097152 | tf_op jit(solution)/shard_map/psum | solution.py:29
  671.9 3.2 copy-start.1
  877.1 9.2 %copy-start.2 = (f32[64,512]{1,0:T(8,128)}, f32[64,512]{1,0:T(8,128)S(1)}, u32[]{:S(2)}) copy-start(f32[64,512]{1,0:T(8,128)S(1)} %fusion.14) | copy-start | bytes 393220
Sparse Core Ops, SparseCore 0:
  236.6 330.4 reduce-scatter.1
  702.2 146.8 all-reduce.1
where the time goes:
time: 899 us; the launch traced here: 893 us
  waiting for transfers between devices  478 us (53%)
  matrix products  232 us (26%)
  local copies, waits for them, and re-layouts  74.5 us (8%)
  blocking collectives  56.4 us (6%)
  other arithmetic  37.9 us (4%)
  between operations  14.4 us (2%)
    reduce_scatter x1, waiting for transfers between devices, body(): lax.psum_scatter(jnp.einsum('qikr,kp->qipr', halfway, factor_three, preci...  331 us
    psum x1, waiting for transfers between devices, body(): gram = lax.psum(local_gram, ('fib', 'row', 'slab'))  147 us
    dot_general x1, matrix products, body(): jnp.einsum('qikr,kp->qipr', halfway, factor_three, precision=highest)  112 us
    all_to_all x1, blocking collectives, body(): lax.all_to_all(summed, 'fib', split_axis=2, concat_axis=1, tiled=True)  56.4 us
    dot_general x1, matrix products, body(): jnp.einsum('ijkr,jq->qikr', reduced, factor_two, precision=highest)  56.3 us
    dot_general x1, local copies, waits for them, and re-layouts, body(): jnp.einsum('ijkr,jq->qikr', reduced, factor_two, precision=highest)  34.8 us
    dot_general x1, matrix products, body(): local_gram = jnp.einsum('qipr,qjpr->ij', fibers, fibers, precision=highest)  27 us
    dot_general x1, matrix products, body(): jnp.einsum('ijkl,lr->ijkr', tensor, factor_four, precision=highest)  26.5 us
  transfers between devices with their start and end apart: 2, of which 2 were waited for; matrix products, arithmetic and copies ran while one was open for 0% of the time, Pallas kernels for 0%

commit v1 on v0

v1 whole, which is shorter than its diff:
```python
import jax
import jax.numpy as jnp
from jax import lax
from jax.sharding import PartitionSpec as P

HIGH = lax.Precision.HIGH
HIGHEST = lax.Precision.HIGHEST


def orthonormal(target):
    result = target
    for repeat in range(2):
        crossed = jnp.dot(result.T, result, precision=HIGHEST)
        cholesky_factor = jnp.linalg.cholesky(crossed)
        result = jax.scipy.linalg.solve_triangular(cholesky_factor, result.T, lower=True).T
    return result


def body(tensor, factor_one, factor_two, factor_three, factor_four):
    two = lax.all_gather(factor_two, "row")
    three = lax.all_gather(factor_three, "slab")
    reduced = jnp.einsum("ijkl,lr->rijk", tensor, factor_four, precision=HIGH)
    exchanged = lax.all_to_all(reduced, ("row", "slab"), split_axis=0, concat_axis=0, tiled=True)
    exchanged = exchanged.reshape(4, 2, 8, 32, 32, 32)
    halfway = jnp.einsum("abrijk,ajq->brikq", exchanged, two, precision=HIGH)
    projected = jnp.einsum("brikq,bkp->priq", halfway, three, precision=HIGH)
    fibers = lax.all_to_all(projected, "fib", split_axis=0, concat_axis=0, tiled=True)
    fibers = fibers.reshape(16, 4, 8, 32, 64)
    one = factor_one.reshape(16, 32, 64)
    crossed = jnp.einsum("fpriq,fia->apqr", fibers, one, precision=HIGH)
    partial = jnp.einsum("fpriq,apqr->fia", fibers, crossed, precision=HIGH)
    target = lax.psum(partial.reshape(512, 64), ("fib", "row", "slab"))
    updated = orthonormal(target)
    core = jnp.einsum("fpriq,fia->aqpr", fibers, updated.reshape(16, 32, 64), precision=HIGH)
    core = lax.all_to_all(core, ("row", "slab"), split_axis=1, concat_axis=3, tiled=True)
    return (updated, core)


def solution(mesh):
    in_specs = (P("fib", "row", "slab", None), P(), P("row", None), P("slab", None), P())
    out_specs = (P(), P(None, ("row", "slab"), "fib", None))
    return jax.shard_map(body, mesh=mesh, in_specs=in_specs, out_specs=out_specs, check_vma=False)
```

time: 899 us -> 618 us (0.69)
  waiting for transfers between devices: 478 us -> 198 us
  matrix products: 232 us -> 85.2 us
  blocking collectives: 56.4 us -> 110 us
  local copies, waits for them, and re-layouts: 74.5 us -> 122 us
  other arithmetic: 37.9 us -> 66.6 us
  starting transfers between devices: 0.08 us -> 13.8 us
    reduce_scatter x1 -> x0, waiting for transfers between devices: 331 us -> none  [body(): lax.psum_scatter(jnp.einsum('qikr,kp->qipr', halfway, factor_three, preci...]
    dot_general x8, matrix products: 232 us -> 83.7 us  [the longest x1 34.2 us: body(): halfway = jnp.einsum('abrijk,ajq->brikq', exchanged, two, precision=HIGH)]
    all_gather x0 -> x2, blocking collectives: none -> 97.1 us  [the longest x1 94.8 us: body(): two = lax.all_gather(factor_two, 'row')]
    all_to_all x0 -> x2, waiting for transfers between devices: none -> 56.4 us  [the longest x1 56.4 us: body(): lax.all_to_all(projected, 'fib', split_axis=0, concat_axis=0, tiled=True)]
    unnamed x13 -> x22, local copies, waits for them, and re-layouts: 25.1 us -> 70.1 us
    all_to_all x1, blocking collectives: 56.4 us -> 13.2 us  [body(): lax.all_to_all(core, ('row', 'slab'), split_axis=1, concat_axis=3, tiled=...]
    all_to_all x1 -> x3, other arithmetic: 13.7 us -> 42.3 us  [the longest x1 26.7 us: body(): lax.all_to_all(reduced, ('row', 'slab'), split_axis=0, concat_axis=0, til...]
    dot_general x3 -> x5, local copies, waits for them, and re-layouts: 35 us -> 50.1 us  [the longest x1 30.4 us: body(): reduced = jnp.einsum('ijkl,lr->rijk', tensor, factor_four, precision=HIGH)]
  transfers between devices with their start and end apart: 2 -> 3, of which waited for: 2 -> 2; matrix products, arithmetic and copies ran while one was open for 0% -> 0% of each run, Pallas kernels for 0% -> 0%
where the time goes in v1:
time: 618 us; the launch traced here: 610 us
  waiting for transfers between devices  198 us (32%)
  local copies, waits for them, and re-layouts  122 us (20%)
  blocking collectives  110 us (18%)
  matrix products  85.2 us (14%)
  other arithmetic  66.6 us (11%)
  between operations  14.5 us (2%)
  starting transfers between devices  13.8 us (2%)
    psum x1, waiting for transfers between devices, body(): target = lax.psum(partial.reshape(512, 64), ('fib', 'row', 'slab'))  141 us
    all_gather x1, blocking collectives, body(): two = lax.all_gather(factor_two, 'row')  94.8 us
    unnamed x22, local copies, waits for them, and re-layouts  70.1 us
    all_to_all x1, waiting for transfers between devices, body(): lax.all_to_all(projected, 'fib', split_axis=0, concat_axis=0, tiled=True)  56.4 us
    dot_general x1, matrix products, body(): halfway = jnp.einsum('abrijk,ajq->brikq', exchanged, two, precision=HIGH)  34.2 us
    dot_general x1, local copies, waits for them, and re-layouts, body(): reduced = jnp.einsum('ijkl,lr->rijk', tensor, factor_four, precision=HIGH)  30.4 us
    all_to_all x1, other arithmetic, body(): lax.all_to_all(reduced, ('row', 'slab'), split_axis=0, concat_axis=0, til...  26.7 us
    dot_general x1, matrix products, body(): reduced = jnp.einsum('ijkl,lr->rijk', tensor, factor_four, precision=HIGH)  13.8 us
  transfers between devices with their start and end apart: 3, of which 2 were waited for; matrix products, arithmetic and copies ran while one was open for 0% of the time, Pallas kernels for 0%

profile of v1, /device:TPU:1, one launch (start us, length us, event | category | flops | bytes accessed | tf_op | source)
XLA Modules:
  0.0 610.0 jit_solution(14929003765516079423)
XLA Ops:
  7.2 0.7 copy-done
  7.9 13.8 %fusion.19 = f32[64,32,32,32]{0,3,2,1:T(8,128)} fusion(f32[32,32,32,128]{3,2,1,0:T(8,128)} %param.8, f32[128,64]{0,1:T(8,128)S(1)} %copy-done), kind=kOutput, calls=%fused_computation.19 | convolution fusion | flops 1610612736 | bytes 25198592 | tf_op jit(solution)/shard_map/ijkl,lr->rijk/dot_general | solution.py:22
  21.7 30.4 %copy.25 = f32[64,32,32,32]{3,2,1,0:T(8,128)} copy(f32[64,32,32,32]{0,3,2,1:T(8,128)} %fusion.19) | data formatting | bytes 16777216 | tf_op jit(solution)/shard_map/ijkl,lr->rijk/dot_general | solution.py:22
  52.1 20.5 %reshape.42 = f32[8,1,262144]{2,1,0:T(1,128)} reshape(f32[64,32,32,32]{3,2,1,0:T(8,128)} %copy.25) | data formatting | bytes 16777216
  72.6 6.9 %all-to-all-start = ((f32[8,1,262144]{2,1,0:T(1,128)}), f32[8,1,262144]{2,1,0:T(1,128)}, u32[]{:S(2)}, u32[]{:S(2)}) async-start(f32[8,1,262144]{2,1,0:T(1,128)} %reshape.42), calls=%async_computation | async-start | bytes 16777216 | tf_op jit(solution)/shard_map/all_to_all | solution.py:23
  79.5 2.3 all-gather.1
  81.8 94.8 %all-gather = f32[128,64]{1,0:T(8,128)S(1)} all-gather(f32[32,64]{1,0:T(8,128)S(1)} %copy-done.6), channel_id=2, replica_groups=mesh['fib'=16,'row'=4,'slab'=2] {'row'}, dimensions={0}, use_global_device_ids=true | all-gather | bytes 40960 | tf_op jit(solution)/shard_map/all_gather | solution.py:20
  177.2 26.7 %reduce.4 = f32[8,262144]{1,0:T(8,128)} reduce(f32[8,1,262144]{2,1,0:T(1,128)} %all-to-all-done, f32[]{:T(128)} %broadcast.36), dimensions={1}, to_apply=%all_to_all.19.reduce_sub_computation | reduce | bytes 16777220 | tf_op jit(solution)/shard_map/all_to_all | solution.py:23
  203.8 25.3 %reshape.43 = f32[64,32,32,32]{3,2,1,0:T(8,128)} reshape(f32[8,262144]{1,0:T(8,128)} %reduce.4) | data formatting | bytes 16777216
  229.1 34.2 %fusion.6 = f32[2,8,32,32,64]{4,3,1,0,2:T(8,128)} fusion(f32[4,32,64,1,1,1]{2,1,4,3,5,0:T(8,128)S(1)} %bitcast.108, f32[4,2,8,32,32,32]{5,4,3,2,1,0:T(8,128)} %bitcast.98), kind=kOutput, calls=%fused_computation.6 | convolution fusion | flops 805306368 | bytes 12615680 | tf_op jit(solution)/shard_map/abrijk,ajq->brikq/dot_general | solution.py:25
  263.3 11.2 %fusion.9 = f32[64,8,32,64]{0,3,2,1:T(8,128)} fusion(f32[2,32,64,1,1]{2,1,0,4,3:T(8,128)S(1)} %bitcast.109, f32[2,8,32,32,64]{4,3,1,0,2:T(8,128)} %fusion.6), kind=kOutput, calls=%fused_computation.7 | convolution fusion | flops 402653184 | bytes 8404992 | tf_op jit(solution)/shard_map/brikq,bkp->priq/dot_general | solution.py:26
  274.5 9.5 %copy.28 = f32[64,8,32,64]{3,2,1,0:T(8,128)} copy(f32[64,8,32,64]{0,3,2,1:T(8,128)} %fusion.9) | data formatting | bytes 8388608 | tf_op jit(solution)/shard_map/brikq,bkp->priq/dot_general | solution.py:26
  284.0 13.3 %reshape.44 = f32[16,1,65536]{2,1,0:T(1,128)} reshape(f32[64,8,32,64]{3,2,1,0:T(8,128)} %copy.28) | data formatting | bytes 8388608
  297.3 6.8 %all-to-all-start.1 = ((f32[16,1,65536]{2,1,0:T(1,128)}), f32[16,1,65536]{2,1,0:T(1,128)}, u32[]{:S(2)}, u32[]{:S(2)}) async-start(f32[16,1,65536]{2,1,0:T(1,128)} %reshape.44), calls=%async_computation.1 | async-start | bytes 8388608 | tf_op jit(solution)/shard_map/all_to_all | solution.py:27
  304.3 56.4 %all-to-all-done.1 = f32[16,1,65536]{2,1,0:T(1,128)} async-done(((f32[16,1,65536]{2,1,0:T(1,128)}), f32[16,1,65536]{2,1,0:T(1,128)}, u32[]{:S(2)}, u32[]{:S(2)}) %all-to-all-start.1) | async-done | bytes 4194336 | tf_op jit(solution)/shard_map/all_to_all | solution.py:27
  360.7 13.7 %reduce.5 = f32[16,65536]{1,0:T(8,128)} reduce(f32[16,1,65536]{2,1,0:T(1,128)} %all-to-all-done.1, f32[]{:T(128)} %broadcast.36), dimensions={1}, to_apply=%all_to_all.20.reduce_sub_computation | reduce | bytes 8388612 | tf_op jit(solution)/shard_map/all_to_all | solution.py:27
  374.4 7.3 %reshape.45 = f32[64,8,32,64]{3,2,1,0:T(8,128)} reshape(f32[16,65536]{1,0:T(8,128)} %reduce.5) | data formatting | bytes 8388608
  381.7 10.1 %copy.29 = f32[16,32,4,64,8]{3,4,2,1,0:T(8,128)S(1)} copy(f32[16,32,4,64,8]{3,1,4,2,0:T(8,128)} %bitcast.99) | data formatting | bytes 8388608 | tf_op jit(solution)/shard_map/fpriq,apqr->fia/dot_general | solution.py:31
  391.8 6.9 %convolution_bitcast_fusion.1 = f32[64,4,64,8]{0,2,3,1:T(8,128)S(1)} fusion(f32[16,4,8,32,64]{4,3,2,1,0:T(8,128)S(1)} %bitcast.101, f32[16,32,64,1,1]{2,1,4,3,0:T(8,128)S(1)} %bitcast.106), kind=kOutput, calls=%fused_computation.9 | convolution fusion | flops 402653184 | bytes 4849664 | tf_op jit(solution)/shard_map/fpriq,fia->apqr/dot_general | solution.py:30
  398.7 9.9 %fusion.12 = f32[512,64]{0,1:T(8,128)} fusion(f32[64,4,64,8]{0,2,3,1:T(8,128)S(1)} %convolution_bitcast_fusion.1, f32[512,4,64,8]{2,3,1,0:T(8,128)S(1)} %bitcast.102), kind=kOutput, calls=%fused_computation.11 | convolution fusion | flops 402653184 | bytes 4849664 | tf_op jit(solution)/shard_map/fpriq,apqr->fia/dot_general | solution.py:31
  408.7 141.3 %all-reduce.2.cloned.1.call-done = f32[512,64]{0,1:T(8,128)} async-done(((f32[512,64]{0,1:T(8,128)}), f32[512,64]{0,1:T(8,128)}) %all-reduce.2.cloned.1.call-update) | async-done | bytes 131088 | tf_op jit(solution)/shard_map/psum | solution.py:32
  549.9 1.2 fusion.27
  551.3 5.8 cholesky.44
  558.4 4.9 custom-call.6
  563.3 1.2 fusion.15
  564.9 6.0 cholesky.55
  572.3 4.9 custom-call.7
  577.7 6.2 %convolution_bitcast_fusion = f32[64,64,4,8]{1,0,3,2:T(8,128)S(1)} fusion(f32[16,32,64,1,1]{2,1,4,3,0:T(8,128)S(1)} %bitcast.107, f32[16,4,8,32,64]{4,3,2,1,0:T(8,128)} %bitcast.100), kind=kOutput, calls=%fused_computation.8 | convolution fusion | flops 402653184 | bytes 4849664 | tf_op jit(solution)/shard_map/fpriq,fia->aqpr/dot_general | solution.py:34
  583.9 0.9 copy.38
  585.5 13.2 %all_to_all.28 = f32[8,1,16384]{2,1,0:T(1,128)S(1)} all-to-all(f32[8,1,16384]{2,1,0:T(1,128)S(1)} %reshape.46), channel_id=1, replica_groups=mesh['fib'=16,'row'=4,'slab'=2] {'row','slab'}, dimensions={0} | all-to-all | bytes 1048576 | tf_op jit(solution)/shard_map/all_to_all | solution.py:35
  598.7 1.9 reduce.6
  601.2 1.8 copy.40
  (34 shorter events, 5.5 us)
Async XLA Ops:
  7.2 0.8 copy-start
  72.6 6.9 %copy-start.5 = (f32[32,64]{1,0:T(8,128)S(1)}, f32[32,64]{1,0:T(8,128)}, u32[]{:S(2)}) copy-start(f32[32,64]{1,0:T(8,128)} %param.11) | copy-start | bytes 24580
  72.6 9.3 %copy-start.6 = (f32[32,64]{1,0:T(8,128)S(1)}, f32[32,64]{1,0:T(8,128)}, u32[]{:S(2)}) copy-start(f32[32,64]{1,0:T(8,128)} %param.10) | copy-start | bytes 24580
  72.6 104.1 %all-to-all-start = ((f32[8,1,262144]{2,1,0:T(1,128)}), f32[8,1,262144]{2,1,0:T(1,128)}, u32[]{:S(2)}, u32[]{:S(2)}) async-start(f32[8,1,262144]{2,1,0:T(1,128)} %reshape.42), calls=%async_computation | async-start | bytes 16777216 | tf_op jit(solution)/shard_map/all_to_all | solution.py:23
  284.0 20.2 %copy-start.4 = (f32[512,64]{0,1:T(8,128)S(1)}, f32[512,64]{0,1:T(8,128)}, u32[]{:S(2)}) copy-start(f32[512,64]{0,1:T(8,128)} %param.9) | copy-start | bytes 393220
  297.3 63.4 %all-to-all-start.1 = ((f32[16,1,65536]{2,1,0:T(1,128)}), f32[16,1,65536]{2,1,0:T(1,128)}, u32[]{:S(2)}, u32[]{:S(2)}) async-start(f32[16,1,65536]{2,1,0:T(1,128)} %reshape.44), calls=%async_computation.1 | async-start | bytes 8388608 | tf_op jit(solution)/shard_map/all_to_all | solution.py:27
  304.1 245.8 %all-reduce.2.cloned.1.call-start = ((), (), s32[]{:S(2)}) async-start(), calls=%async_computation.3 | async-start | bytes 262144 | tf_op jit(solution)/shard_map/psum | solution.py:32
  381.7 10.1 %copy-start.2 = (f32[64,8,32,64]{3,2,1,0:T(8,128)S(1)}, f32[64,8,32,64]{3,2,1,0:T(8,128)}, u32[]{:S(2)}) copy-start(f32[64,8,32,64]{3,2,1,0:T(8,128)} %reshape.45) | copy-start | bytes 12582916
  577.6 23.5 %copy-start.3 = (f32[512,64]{0,1:T(8,128)}, f32[512,64]{0,1:T(8,128)S(1)}, u32[]{:S(2)}) copy-start(f32[512,64]{0,1:T(8,128)S(1)} %convolution_bitcast_fusion.2) | copy-start | bytes 393220
  577.7 25.2 %copy-start.1 = (f32[128,64]{0,1:T(8,128)S(1)}, f32[128,64]{0,1:T(8,128)}, u32[]{:S(2)}) copy-start(f32[128,64]{0,1:T(8,128)} %param.12) | copy-start | bytes 98308
Sparse Core Ops, SparseCore 0:
  408.8 141.1 all-reduce.1

commit v2 on v1

v2 whole, which is shorter than its diff:
```python
import jax
import jax.numpy as jnp
from jax import lax
from jax.experimental import pallas as pl
from jax.experimental.pallas import tpu as pltpu
from jax.sharding import PartitionSpec as P

HIGHEST = lax.Precision.HIGHEST
MESH = pl.DeviceIdType.MESH
F32 = jnp.float32
BF16 = jnp.bfloat16
CHUNKS = 8
LAG = 2


def split(x):
    high = x.astype(BF16)
    return high, (x - high.astype(F32)).astype(BF16)


def dot(a, b):
    return jnp.dot(a, b, preferred_element_type=F32)


def dot_nt(a, b):
    return lax.dot_general(a, b, (((1,), (1,)), ((), ())), preferred_element_type=F32)


def place():
    return lax.axis_index("fib"), lax.axis_index("row"), lax.axis_index("slab")


def plane_peer(d):
    fib, row, slab = place()
    row, slab = lax.rem(row + d // 2, 4), lax.rem(slab + d % 2, 2)
    return (fib, row, slab), row * 2 + slab


def fib_peer(d):
    fib, row, slab = place()
    fib = lax.rem(fib // 4 + d // 4, 4) * 4 + lax.rem(fib % 4 + d % 4, 4)
    return (fib, row, slab), fib


def each(lower, upper, step):
    def run(index, carry):
        step(index)
        return carry

    lax.fori_loop(lower, upper, run, 0)


def remote(src, dst, send, recv, device):
    return pltpu.make_async_remote_copy(
        src_ref=src, dst_ref=dst, send_sem=send, recv_sem=recv, device_id=device, device_id_type=MESH
    )


def greet(plane, fibers):
    barrier = pltpu.get_barrier_semaphore()
    count = 0
    if plane:
        count += 7
        each(1, 8, lambda d: pl.semaphore_signal(barrier, inc=1, device_id=plane_peer(d)[0], device_id_type=MESH))
    if fibers:
        count += 15
        each(1, 16, lambda d: pl.semaphore_signal(barrier, inc=1, device_id=fib_peer(d)[0], device_id_type=MESH))
    pl.semaphore_wait(barrier, count)


def stack(x):
    high, low = split(x)
    return jnp.concatenate([jnp.concatenate([high, high], 1), jnp.concatenate([low, low], 1)], 0)


def left_half(shape):
    return lax.broadcasted_iota(jnp.int32, shape, 1) < 64


def rows_of(fibers, column):
    return jnp.concatenate([fibers[half, pl.ds(column, 128, stride=32), :] for half in range(2)], axis=1)


def fold(out):
    left = left_half((64, 128))
    folded = jnp.where(left, out[0:64, 0:128], out[64:128, 0:128])
    folded = folded + jnp.where(left, out[128:192, 128:256], out[192:256, 128:256])
    return folded + pltpu.roll(folded, 64, 1)


def project_kernel(
    tensor, four, three, two, one, target, fibers_out, four_stack, one_stack,
    staged, outgoing, incoming, halfway, contracted, fibers, two_all, three_all, wide_high, wide_low,
    crossed, partial, scattered, shared, reduced,
    load_sem, own_sem, z_send, z_recv, fib_own_sem, f_send, f_recv,
    two_send, two_recv, three_send, three_recv, small_own, rs_send, rs_recv, ar_send, ar_recv, ag_send, ag_recv, out_sem,
):
    fib, row, slab = place()
    me = row * 2 + slab

    def load(chunk):
        return pltpu.make_async_copy(tensor.at[chunk], staged.at[chunk % 3], load_sem.at[chunk % 3])

    load(0).start()
    load(1).start()
    four_stack[...] = stack(four[...])
    one_stack[...] = stack(one[...])
    greet(True, True)

    def two_copy(step, block):
        peer = lax.rem(row + step, 4)
        return remote(two, two_all.at[block], two_send.at[step], two_recv.at[block], (fib, peer, slab))

    def three_copy():
        return remote(three, three_all.at[slab], three_send, three_recv, (fib, row, 1 - slab))

    two_own = pltpu.make_async_copy(two, two_all.at[row], small_own.at[0])
    three_own = pltpu.make_async_copy(three, three_all.at[slab], small_own.at[1])
    each(1, 4, lambda s: two_copy(s, row).start())
    three_copy().start()
    two_own.start()
    three_own.start()

    def z_copy(chunk, d):
        device, peer = plane_peer(d)
        return remote(
            outgoing.at[chunk, pl.ds(peer * 256, 256), :],
            incoming.at[chunk, pl.ds(me * 256, 256), :],
            z_send.at[chunk, d], z_recv.at[chunk, me], device,
        )

    def z_arrived(chunk, d):
        device, peer = plane_peer(d)
        block = incoming.at[chunk, pl.ds(peer * 256, 256), :]
        remote(block, block, z_send.at[chunk, d], z_recv.at[chunk, peer], device).wait_recv()

    def z_own(chunk):
        rows = pl.ds(me * 256, 256)
        return pltpu.make_async_copy(outgoing.at[chunk, rows, :], incoming.at[chunk, rows, :], own_sem.at[chunk])

    def f_copy(chunk, d):
        device, peer = fib_peer(d)
        return remote(
            contracted.at[chunk, :, pl.ds(peer * 32, 32), :],
            fibers.at[:, pl.ds((fib * CHUNKS + chunk) * 32, 32), :],
            f_send.at[chunk, d], f_recv.at[chunk, fib], device,
        )

    def f_arrived(chunk, d):
        device, peer = fib_peer(d)
        block = fibers.at[:, pl.ds((peer * CHUNKS + chunk) * 32, 32), :]
        remote(block, block, f_send.at[chunk, d], f_recv.at[chunk, peer], device).wait_recv()

    def f_own(chunk):
        return pltpu.make_async_copy(
            contracted.at[chunk, :, pl.ds(fib * 32, 32), :],
            fibers.at[:, pl.ds((fib * CHUNKS + chunk) * 32, 32), :],
            fib_own_sem.at[chunk],
        )

    def mode_four(chunk):
        slot = chunk % 3

        def two_steps(pair):
            first = staged[slot, pl.ds(2 * pair, 128, stride=32), :]
            second = staged[slot, pl.ds(2 * pair + 1, 128, stride=32), :]
            high, low = split(jnp.concatenate([first, second], axis=0))
            out = dot_nt(four_stack[...], jnp.concatenate([high, low], axis=1))
            out = out[:64] + out[64:]
            outgoing[chunk, pl.ds(2 * pair, 64, stride=32), :] = out[:, :128]
            outgoing[chunk, pl.ds(2 * pair + 1, 64, stride=32), :] = out[:, 128:]

        each(0, 16, two_steps)

    def modes_three_two(chunk):
        whole = three_all[0] + three_all[1]
        high, low = split(whole)
        lanes = lax.broadcasted_iota(jnp.int32, (64, 256), 1)
        factor = jnp.where(lanes < 128, high.astype(F32), low.astype(F32)).astype(BF16)

        def rank(r):
            parts = []
            for z in range(4):
                pieces = [incoming[chunk, pl.ds((2 * z + c) * 256 + r * 32, 32), :] for c in range(2)]
                high, low = split(jnp.concatenate(pieces, axis=0))
                parts.append(jnp.concatenate([high, low, high, low], axis=0))
            out = dot(factor, jnp.concatenate(parts, axis=1))
            for z in range(4):
                halfway[z, pl.ds(r, 64, stride=8), :] = out[:, z * 128 : (z + 1) * 128]

        each(0, 8, rank)

        def rows(block):
            at = pl.ds(pl.multiple_of(block * 128, 128), 128)
            total = jnp.zeros((128, 256), F32)
            for z in range(4):
                high, low = split(halfway[z, at, :])
                both = dot(jnp.concatenate([high, low], axis=0), wide_high[z])
                total = total + both[:128] + both[128:] + dot(high, wide_low[z])
            contracted[chunk, 0, at, :] = total[:, :128]
            contracted[chunk, 1, at, :] = total[:, 128:]

        each(0, 4, rows)

    def widen():
        two_own.wait()
        three_own.wait()
        each(1, 4, lambda s: two_copy(s, lax.rem(row + 4 - s, 4)).wait_recv())
        remote(three, three_all.at[1 - slab], three_send, three_recv, (fib, row, 1 - slab)).wait_recv()
        left = left_half((32, 128))
        nothing = jnp.zeros((32, 128), F32)
        for z in range(4):
            block = two_all[z]
            sides = (jnp.where(left, block, 0.0), jnp.where(left, 0.0, block))
            pieces = []
            for i in range(4):
                tiles = [nothing, nothing]
                tiles[i // 2] = sides[i % 2]
                pieces.append(jnp.concatenate(tiles, axis=1))
            high, low = split(jnp.concatenate(pieces, axis=0))
            wide_high[z] = high
            wide_low[z] = low

    def advance(turn):
        @pl.when(turn < CHUNKS)
        def _():
            load(turn).wait()

            @pl.when(turn + 2 < CHUNKS)
            def _():
                load(turn + 2).start()

            mode_four(turn)

            @pl.when(turn >= 2)
            def _():
                each(1, 8, lambda d: z_copy(turn - 2, d).wait_send())

            each(1, 8, lambda d: z_copy(turn, d).start())
            z_own(turn).start()

        @pl.when(turn == 0)
        def _():
            widen()

        @pl.when(turn >= LAG)
        def _():
            chunk = turn - LAG
            z_own(chunk).wait()
            each(1, 8, lambda d: z_arrived(chunk, d))
            modes_three_two(chunk)
            each(1, 16, lambda d: f_copy(chunk, d).start())
            f_own(chunk).start()

    each(0, CHUNKS + LAG, advance)
    each(CHUNKS - 2, CHUNKS, lambda chunk: each(1, 8, lambda d: z_copy(chunk, d).wait_send()))

    def gathered(chunk):
        f_own(chunk).wait()
        each(1, 16, lambda d: f_arrived(chunk, d))

    each(0, CHUNKS, gathered)
    out_copy = pltpu.make_async_copy(fibers, fibers_out, out_sem)
    out_copy.start()

    def cross(column):
        high, low = split(rows_of(fibers, column))
        out = dot(one_stack[...], jnp.concatenate([high, low], axis=0))
        crossed[column] = fold(out[:256] + out[256:])

    each(0, 32, cross)

    partial[...] = jnp.zeros_like(partial)

    def back(column):
        high, low = split(rows_of(fibers, column))
        left = left_half((64, 128))
        block = crossed[column]
        nothing = jnp.zeros((64, 128), F32)
        sides = (jnp.where(left, block, 0.0), jnp.where(left, 0.0, block))
        wide = jnp.concatenate(
            [
                jnp.concatenate([sides[0], nothing], axis=1),
                jnp.concatenate([sides[1], nothing], axis=1),
                jnp.concatenate([nothing, sides[0]], axis=1),
                jnp.concatenate([nothing, sides[1]], axis=1),
            ],
            axis=0,
        )
        wide_h, wide_l = split(wide)
        both = dot_nt(jnp.concatenate([high, low], axis=0), wide_h)
        partial[...] += both[:128] + both[128:] + dot_nt(high, wide_l)

    each(0, 32, back)

    def rs_copy(d):
        device, peer = plane_peer(d)
        return remote(partial.at[pl.ds(peer * 16, 16), :], scattered.at[me], rs_send.at[d], rs_recv.at[me], device)

    def rs_arrived(d):
        device, peer = plane_peer(d)
        remote(scattered.at[peer], scattered.at[peer], rs_send.at[d], rs_recv.at[peer], device).wait_recv()

    def ar_copy(d):
        device, peer = fib_peer(d)
        return remote(shared.at[fib], shared.at[fib], ar_send.at[d], ar_recv.at[fib], device)

    def ar_arrived(d):
        device, peer = fib_peer(d)
        remote(shared.at[peer], shared.at[peer], ar_send.at[d], ar_recv.at[peer], device).wait_recv()

    def ag_copy(d):
        device, peer = plane_peer(d)
        mine = reduced.at[pl.ds(me * 16, 16), :]
        return remote(mine, mine, ag_send.at[d], ag_recv.at[me], device)

    def ag_arrived(d):
        device, peer = plane_peer(d)
        block = reduced.at[pl.ds(peer * 16, 16), :]
        remote(block, block, ag_send.at[d], ag_recv.at[peer], device).wait_recv()

    each(1, 8, lambda d: rs_copy(d).start())
    scattered[me] = partial[pl.ds(pl.multiple_of(me * 16, 16), 16), :]
    each(1, 8, rs_arrived)
    shared[fib] = jnp.sum(scattered[...], axis=0)
    each(1, 16, lambda d: ar_copy(d).start())
    each(1, 16, ar_arrived)
    reduced[pl.ds(pl.multiple_of(me * 16, 16), 16), :] = jnp.sum(shared[...], axis=0)
    each(1, 8, lambda d: ag_copy(d).start())
    each(1, 8, ag_arrived)
    target[...] = reduced[...]

    each(1, 8, lambda d: rs_copy(d).wait_send())
    each(1, 16, lambda d: ar_copy(d).wait_send())
    each(1, 8, lambda d: ag_copy(d).wait_send())
    each(1, 4, lambda s: two_copy(s, row).wait_send())
    three_copy().wait_send()
    each(0, CHUNKS, lambda chunk: each(1, 16, lambda d: f_copy(chunk, d).wait_send()))
    out_copy.wait()


def core_kernel(updated, fibers, gathered, stacked, outgoing, incoming, send, recv):
    fib, row, slab = place()
    me = row * 2 + slab
    stacked[...] = stack(updated[...])
    greet(True, False)

    def project(group):
        folded = []
        for s in range(4):
            high, low = split(rows_of(fibers, group * 4 + s))
            out = dot(stacked[...], jnp.concatenate([high, low], axis=0))
            folded.append(fold(out[:256] + out[256:]))
        left = left_half((64, 128))
        square = jnp.concatenate(
            [jnp.where(left, folded[0], folded[1]), jnp.where(left, folded[2], folded[3])], axis=0
        )
        turned = square.T
        for half in range(2):
            for peer in range(8):
                start = half * 64 + peer * 8
                at = pl.ds(pl.multiple_of(group * 16 + half * 8, 8), 8)
                outgoing[peer, at, :] = turned[start : start + 8, :]

    each(0, 8, project)

    def copy(d):
        device, peer = plane_peer(d)
        return remote(outgoing.at[peer], incoming.at[me], send.at[d], recv.at[me], device)

    def arrived(d):
        device, peer = plane_peer(d)
        remote(incoming.at[peer], incoming.at[peer], send.at[d], recv.at[peer], device).wait_recv()

    each(1, 8, lambda d: copy(d).start())
    incoming[me] = outgoing[me]
    each(1, 8, arrived)
    gathered[...] = incoming[...]
    each(1, 8, lambda d: copy(d).wait_send())


def turned(matrix):
    return matrix.reshape(128, 4, 64).transpose(1, 2, 0).reshape(256, 128)


def orthonormal(target):
    result = target
    for repeat in range(2):
        crossed = jnp.dot(result.T, result, precision=HIGHEST)
        cholesky_factor = jnp.linalg.cholesky(crossed)
        result = jax.scipy.linalg.solve_triangular(cholesky_factor, result.T, lower=True).T
    return result


def body(tensor, factor_one, factor_two, factor_three, factor_four):
    slab = lax.axis_index("slab")
    across = factor_three.T
    nothing = jnp.zeros_like(across)
    three = jnp.where(slab == 0, jnp.concatenate([across, nothing], 1), jnp.concatenate([nothing, across], 1))
    three = jnp.concatenate([three] * 4, 1)
    two = jnp.concatenate([factor_two, factor_two], 1)
    vmem = pl.BlockSpec(memory_space=pltpu.VMEM)
    hbm = pl.BlockSpec(memory_space=pl.ANY)
    dma = pltpu.SemaphoreType.DMA
    target, fibers = pl.pallas_call(
        project_kernel,
        out_shape=(jax.ShapeDtypeStruct((128, 256), F32), jax.ShapeDtypeStruct((2, 4096, 128), F32)),
        in_specs=[hbm, vmem, vmem, vmem, vmem],
        out_specs=(vmem, hbm),
        scratch_shapes=[
            pltpu.VMEM((128, 256), BF16),
            pltpu.VMEM((512, 256), BF16),
            pltpu.VMEM((3, 4096, 128), F32),
            pltpu.VMEM((CHUNKS, 2048, 128), F32),
            pltpu.VMEM((CHUNKS, 2048, 128), F32),
            pltpu.VMEM((4, 512, 128), F32),
            pltpu.VMEM((CHUNKS, 2, 512, 128), F32),
            pltpu.VMEM((2, 4096, 128), F32),
            pltpu.VMEM((4, 32, 128), F32),
            pltpu.VMEM((2, 64, 256), F32),
            pltpu.VMEM((4, 128, 256), BF16),
            pltpu.VMEM((4, 128, 256), BF16),
            pltpu.VMEM((32, 64, 128), F32),
            pltpu.VMEM((128, 256), F32),
            pltpu.VMEM((8, 16, 256), F32),
            pltpu.VMEM((16, 16, 256), F32),
            pltpu.VMEM((128, 256), F32),
            dma((3,)), dma((CHUNKS,)), dma((CHUNKS, 8)), dma((CHUNKS, 8)), dma((CHUNKS,)), dma((CHUNKS, 16)), dma((CHUNKS, 16)),
            dma((4,)), dma((4,)), dma(()), dma(()), dma((2,)), dma((8,)), dma((8,)), dma((16,)), dma((16,)), dma((8,)), dma((8,)), dma(()),
        ],
        compiler_params=pltpu.CompilerParams(collective_id=0, has_side_effects=True, vmem_limit_bytes=52 * 2**20),
        name="project",
    )(tensor.reshape(8, 4096, 128), factor_four.T, three, two, turned(factor_one))
    updated = orthonormal(target.reshape(512, 64))
    core = pl.pallas_call(
        core_kernel,
        out_shape=jax.ShapeDtypeStruct((8, 128, 128), F32),
        in_specs=[vmem, vmem],
        out_specs=vmem,
        scratch_shapes=[pltpu.VMEM((512, 256), BF16), pltpu.VMEM((8, 128, 128), F32), pltpu.VMEM((8, 128, 128), F32), dma((8,)), dma((8,))],
        compiler_params=pltpu.CompilerParams(collective_id=1, has_side_effects=True, vmem_limit_bytes=32 * 2**20),
        name="core",
    )(turned(updated), fibers)
    core = core.reshape(8, 4, 2, 2, 8, 2, 64).transpose(6, 4, 1, 0, 2, 5, 3).reshape(64, 8, 4, 64)
    return (updated, core)


def solution(mesh):
    in_specs = (P("fib", "row", "slab", None), P(), P("row", None), P("slab", None), P())
    out_specs = (P(), P(None, ("row", "slab"), "fib", None))
    return jax.shard_map(body, mesh=mesh, in_specs=in_specs, out_specs=out_specs, check_vma=False)
```

time: 618 us -> 214 us (0.35); the launches traced: 610 us -> 213 us
  waiting for transfers between devices: 198 us -> 0 us
  Pallas kernels: 0 us -> 178 us
  local copies, waits for them, and re-layouts: 122 us -> 7.97 us
  blocking collectives: 110 us -> 0 us
  matrix products: 85.2 us -> 1.63 us
  other arithmetic: 66.6 us -> 25.2 us
  starting transfers between devices: 13.8 us -> 0 us
  between operations: 14.5 us -> 0.8 us
    pallas_call x0 -> x2, Pallas kernels: none -> 178 us  [the longest x1 161 us: body(): pl.pallas_call(project_kernel, out_shape=(jax.ShapeDtypeStruct((128, 256)...]
    psum x1 -> x0, waiting for transfers between devices: 141 us -> none  [body(): target = lax.psum(partial.reshape(512, 64), ('fib', 'row', 'slab'))]
    all_gather x2 -> x0, blocking collectives: 97.1 us -> none  [the longest x1 94.8 us: body(): two = lax.all_gather(factor_two, 'row')]
    dot_general x6 -> x0, matrix products: 82.2 us -> none  [the longest x1 34.2 us: body(): halfway = jnp.einsum('abrijk,ajq->brikq', exchanged, two, precision=HIGH)]
    unnamed x22 -> x9, local copies, waits for them, and re-layouts: 70.1 us -> 6.66 us
    all_to_all x2 -> x0, waiting for transfers between devices: 56.4 us -> none  [the longest x1 56.4 us: body(): lax.all_to_all(projected, 'fib', split_axis=0, concat_axis=0, tiled=True)]
    dot_general x3 -> x0, local copies, waits for them, and re-layouts: 49.9 us -> none  [the longest x1 30.4 us: body(): reduced = jnp.einsum('ijkl,lr->rijk', tensor, factor_four, precision=HIGH)]
    all_to_all x3 -> x0, other arithmetic: 42.3 us -> none  [the longest x1 26.7 us: body(): lax.all_to_all(reduced, ('row', 'slab'), split_axis=0, concat_axis=0, til...]
  transfers between devices with their start and end apart: 3 -> 0, of which waited for: 2 -> 0; matrix products, arithmetic and copies ran while one was open for 0% -> 0% of each run, Pallas kernels for 0% -> 0%
where the time goes in v2:
time: 214 us; the launch traced here: 213 us
  Pallas kernels  178 us (83%)
  other arithmetic  25.2 us (12%)
  local copies, waits for them, and re-layouts  7.97 us (4%)
    pallas_call x1, Pallas kernels, body(): pl.pallas_call(project_kernel, out_shape=(jax.ShapeDtypeStruct((128, 256)...  161 us
    pallas_call x1, Pallas kernels, body(): pl.pallas_call(core_kernel, out_shape=jax.ShapeDtypeStruct((8, 128, 128),...  16.6 us
    another operation x6, other arithmetic, orthonormal(): cholesky_factor = jnp.linalg.cholesky(crossed)  13 us
    another operation x4, other arithmetic, orthonormal(): jax.scipy.linalg.solve_triangular(cholesky_factor, result.T, lower=True)  11.1 us
    unnamed x9, local copies, waits for them, and re-layouts  6.66 us

profile of v2, /device:TPU:1, one launch (start us, length us, event | category | flops | bytes accessed | tf_op | source)
XLA Modules:
  0.0 213.2 jit_solution(10341927798655913410)
XLA Ops:
  0.6 0.9 pad_maximum_fusion.1.two
  1.5 0.8 copy.13
  2.3 0.1 pad_select_fusion
  2.4 0.1 pad_maximum_fusion.three
  2.5 1.0 copy.14
  3.5 0.1 copy.15
  3.6 0.0 copy-start.1
  3.7 0.8 copy-done.1
  4.4 161.0 %project.1 = (f32[128,256]{1,0:T(8,128)S(1)}, f32[2,4096,128]{2,1,0:T(8,128)}) custom-call(f32[8,4096,128]{2,1,0:T(8,128)} %bitcast.45, f32[64,128]{1,0:T(8,128)S(1)} %bitcast.44, f32[64,256]{1,0:T(8,128)S(1)} %pad_maximum_fusion.three, f32[32,128]{1,0:T(8,128)S(1)} %pad_maximum_fusion.1.two, f32[256,128]{1,0:T(8,128)S(1)} %bitcast.42), custom_call_target="tpu_custom_call" | custom-call | tf_op jit(solution)/shard_map/project/pallas_call | solution.py:405
  165.5 0.1 reshape.39
  165.6 0.6 fusion.10
  166.2 0.1 copy.16
  166.3 5.8 %cholesky.44 = f32[64,64]{1,0:T(8,128)S(1)} custom-call(f32[64,64]{1,0:T(8,128)S(1)} %fusion.7), custom_call_target="Cholesky" | custom-call | tf_op jit(solution)/shard_map/jit(cholesky)/cholesky | solution.py:390
  172.1 0.6 compare_reduce_fusion.1
  172.8 0.7 fusion.2
  173.4 4.9 %custom-call.6 = f32[1,64,64]{1,2,0:T(8,128)S(1)} custom-call(f32[1,64,64]{2,1,0:T(8,128)S(1)} %fusion.2), custom_call_target="InvertDiagBlocksLowerTriangular" | custom-call | tf_op jit(solution)/shard_map/jit(_solve_triangular)/triangular_solve | solution.py:391
  178.3 0.4 fusion
  178.8 0.3 fusion.11
  179.1 0.1 copy.17
  179.2 5.8 %cholesky.55 = f32[64,64]{1,0:T(8,128)S(1)} custom-call(f32[64,64]{1,0:T(8,128)S(1)} %fusion.5), custom_call_target="Cholesky" | custom-call | tf_op jit(solution)/shard_map/jit(cholesky)/cholesky | solution.py:390
  185.0 0.6 compare_reduce_fusion
  185.7 0.7 fusion.3
  186.3 4.9 %custom-call.7 = f32[1,64,64]{1,2,0:T(8,128)S(1)} custom-call(f32[1,64,64]{2,1,0:T(8,128)S(1)} %fusion.3), custom_call_target="InvertDiagBlocksLowerTriangular" | custom-call | tf_op jit(solution)/shard_map/jit(_solve_triangular)/triangular_solve | solution.py:391
  191.2 0.3 convolution_bitcast_fusion
  191.6 0.1 copy.18
  191.7 0.1 copy.19
  191.8 0.0 copy-start
  191.9 2.2 %copy-done = f32[2,4096,128]{2,1,0:T(8,128)S(1)} copy-done((f32[2,4096,128]{2,1,0:T(8,128)S(1)}, f32[2,4096,128]{2,1,0:T(8,128)}, u32[]{:S(2)}) %copy-start) | copy-done | bytes 4194328
  194.0 16.6 %core.1 = f32[8,128,128]{2,1,0:T(8,128)S(1)} custom-call(f32[256,128]{1,0:T(8,128)S(1)} %bitcast.43, f32[2,4096,128]{2,1,0:T(8,128)S(1)} %copy-done), custom_call_target="tpu_custom_call" | custom-call | tf_op jit(solution)/shard_map/core/pallas_call | solution.py:435
  210.6 0.6 reshape.42
  211.2 0.1 copy.20
  211.3 1.9 copy.21
  (6 shorter events, 0.1 us)
Async XLA Ops:
  3.6 0.8 copy-start.1
  191.6 21.6 %copy-start.2 = (f32[512,64]{0,1:T(8,128)}, f32[512,64]{0,1:T(8,128)S(1)}, u32[]{:S(2)}) copy-start(f32[512,64]{0,1:T(8,128)S(1)} %convolution_bitcast_fusion) | copy-start | bytes 393220
  191.8 2.2 %copy-start = (f32[2,4096,128]{2,1,0:T(8,128)S(1)}, f32[2,4096,128]{2,1,0:T(8,128)}, u32[]{:S(2)}) copy-start(f32[2,4096,128]{2,1,0:T(8,128)} %get-tuple-element.7.fibers) | copy-start | bytes 12582916

commit v3 on v2

--- a/solution.py
+++ b/solution.py
@@ -77,23 +77,34 @@
     return lax.broadcasted_iota(jnp.int32, shape, 1) < 64
 
 
-def rows_of(fibers, column):
-    return jnp.concatenate([fibers[half, pl.ds(column, 128, stride=32), :] for half in range(2)], axis=1)
-
-
-def fold(out):
-    left = left_half((64, 128))
-    folded = jnp.where(left, out[0:64, 0:128], out[64:128, 0:128])
-    folded = folded + jnp.where(left, out[128:192, 128:256], out[192:256, 128:256])
-    return folded + pltpu.roll(folded, 64, 1)
-
-
-def project_kernel(
-    tensor, four, three, two, one, target, fibers_out, four_stack, one_stack,
+def halves(x):
+    return jnp.concatenate(split(x), axis=0)
+
+
+def eliminate(crossed):
+    lane = lax.broadcasted_iota(jnp.int32, (8, 64), 1)
+    row = lax.broadcasted_iota(jnp.int32, (8, 64), 0)
+    below = lax.broadcasted_iota(jnp.int32, (8, 128), 0)
+    blocks = [
+        jnp.concatenate([crossed[8 * b : 8 * b + 8], jnp.where(lane == row + 8 * b, 1.0, 0.0)], axis=1) for b in range(8)
+    ]
+    for j in range(64):
+        b, k = j // 8, j % 8
+        scale = lax.rsqrt(blocks[b][k : k + 1, j : j + 1])
+        pivot = blocks[b][k : k + 1, :] * scale
+        updated = blocks[b] - blocks[b][:, j : j + 1] * scale * pivot
+        for other in range(b + 1, 8):
+            blocks[other] = blocks[other] - blocks[other][:, j : j + 1] * scale * pivot
+        blocks[b] = jnp.where(below > k, updated, jnp.where(below == k, pivot, blocks[b]))
+    return jnp.concatenate(blocks, axis=0)[:, 64:]
+
+
+def kernel(
+    tensor, four, three, two, one, updated, collected, four_stack, one_stack,
     staged, outgoing, incoming, halfway, contracted, fibers, two_all, three_all, wide_high, wide_low,
-    crossed, partial, scattered, shared, reduced,
+    fibers_high, fibers_low, partial, scattered, shared, reduced, core_out, core_in,
     load_sem, own_sem, z_send, z_recv, fib_own_sem, f_send, f_recv,
-    two_send, two_recv, three_send, three_recv, small_own, rs_send, rs_recv, ar_send, ar_recv, ag_send, ag_recv, out_sem,
+    two_send, two_recv, three_send, three_recv, small_own, rs_send, rs_recv, ar_send, ar_recv, ag_send, ag_recv, core_send, core_recv,
 ):
     fib, row, slab = place()
     me = row * 2 + slab
@@ -104,7 +115,7 @@
     load(0).start()
     load(1).start()
     four_stack[...] = stack(four[...])
-    one_stack[...] = stack(one[...])
+    one_stack[...] = halves(one[...])
     greet(True, True)
 
     def two_copy(step, block):
@@ -141,20 +152,20 @@
     def f_copy(chunk, d):
         device, peer = fib_peer(d)
         return remote(
-            contracted.at[chunk, :, pl.ds(peer * 32, 32), :],
-            fibers.at[:, pl.ds((fib * CHUNKS + chunk) * 32, 32), :],
+            contracted.at[chunk, pl.ds(peer * 64, 64), :],
+            fibers.at[pl.ds((fib * CHUNKS + chunk) * 64, 64), :],
             f_send.at[chunk, d], f_recv.at[chunk, fib], device,
         )
 
     def f_arrived(chunk, d):
         device, peer = fib_peer(d)
-        block = fibers.at[:, pl.ds((peer * CHUNKS + chunk) * 32, 32), :]
+        block = fibers.at[pl.ds((peer * CHUNKS + chunk) * 64, 64), :]
         remote(block, block, f_send.at[chunk, d], f_recv.at[chunk, peer], device).wait_recv()
 
     def f_own(chunk):
         return pltpu.make_async_copy(
-            contracted.at[chunk, :, pl.ds(fib * 32, 32), :],
-            fibers.at[:, pl.ds((fib * CHUNKS + chunk) * 32, 32), :],
+            contracted.at[chunk, pl.ds(fib * 64, 64), :],
+            fibers.at[pl.ds((fib * CHUNKS + chunk) * 64, 64), :],
             fib_own_sem.at[chunk],
         )
 
@@ -197,8 +208,15 @@
                 high, low = split(halfway[z, at, :])
                 both = dot(jnp.concatenate([high, low], axis=0), wide_high[z])
                 total = total + both[:128] + both[128:] + dot(high, wide_low[z])
-            contracted[chunk, 0, at, :] = total[:, :128]
-            contracted[chunk, 1, at, :] = total[:, 128:]
+            left = left_half((16, 128))
+            for f in range(4):
+                for t in range(2):
+                    lower = total[f * 32 : f * 32 + 16, t * 128 : t * 128 + 128]
+                    upper = total[f * 32 + 16 : f * 32 + 32, t * 128 : t * 128 + 128]
+                    even = jnp.where(left, lower, pltpu.roll(upper, 64, 1))
+                    odd = jnp.where(left, pltpu.roll(lower, 64, 1), upper)
+                    start = pl.multiple_of((block * 4 + f) * 64 + t * 32, 32)
+                    contracted[chunk, pl.ds(start, 32), :] = jnp.concatenate([even, odd], axis=0)
 
         each(0, 4, rows)
 
@@ -260,42 +278,23 @@
         each(1, 16, lambda d: f_arrived(chunk, d))
 
     each(0, CHUNKS, gathered)
-    out_copy = pltpu.make_async_copy(fibers, fibers_out, out_sem)
-    out_copy.start()
-
-    def cross(column):
-        high, low = split(rows_of(fibers, column))
-        out = dot(one_stack[...], jnp.concatenate([high, low], axis=0))
-        crossed[column] = fold(out[:256] + out[256:])
-
-    each(0, 32, cross)
-
     partial[...] = jnp.zeros_like(partial)
 
-    def back(column):
-        high, low = split(rows_of(fibers, column))
-        left = left_half((64, 128))
-        block = crossed[column]
-        nothing = jnp.zeros((64, 128), F32)
-        sides = (jnp.where(left, block, 0.0), jnp.where(left, 0.0, block))
-        wide = jnp.concatenate(
-            [
-                jnp.concatenate([sides[0], nothing], axis=1),
-                jnp.concatenate([sides[1], nothing], axis=1),
-                jnp.concatenate([nothing, sides[0]], axis=1),
-                jnp.concatenate([nothing, sides[1]], axis=1),
-            ],
-            axis=0,
-        )
-        wide_h, wide_l = split(wide)
-        both = dot_nt(jnp.concatenate([high, low], axis=0), wide_h)
-        partial[...] += both[:128] + both[128:] + dot_nt(high, wide_l)
-
-    each(0, 32, back)
+    def cross(step):
+        block = jnp.concatenate([fibers[pl.ds(2 * step + n, 512, stride=16), :] for n in range(2)], axis=1)
+        high, low = split(block)
+        fibers_high[step] = high
+        fibers_low[step] = low
+        both = dot(one_stack[...], high)
+        both_parts = halves(both[:64] + both[64:] + dot(one_stack[:64, :], low))
+        back = dot_nt(both_parts, high)
+        partial[...] += back[:64] + back[64:] + dot_nt(both_parts[:64], low)
+
+    each(0, 8, cross)
 
     def rs_copy(d):
         device, peer = plane_peer(d)
-        return remote(partial.at[pl.ds(peer * 16, 16), :], scattered.at[me], rs_send.at[d], rs_recv.at[me], device)
+        return remote(partial.at[pl.ds(peer * 8, 8), :], scattered.at[me], rs_send.at[d], rs_recv.at[me], device)
 
     def rs_arrived(d):
         device, peer = plane_peer(d)
@@ -311,24 +310,59 @@
 
     def ag_copy(d):
         device, peer = plane_peer(d)
-        mine = reduced.at[pl.ds(me * 16, 16), :]
+        mine = reduced.at[pl.ds(me * 8, 8), :]
         return remote(mine, mine, ag_send.at[d], ag_recv.at[me], device)
 
     def ag_arrived(d):
         device, peer = plane_peer(d)
-        block = reduced.at[pl.ds(peer * 16, 16), :]
+        block = reduced.at[pl.ds(peer * 8, 8), :]
         remote(block, block, ag_send.at[d], ag_recv.at[peer], device).wait_recv()
 
     each(1, 8, lambda d: rs_copy(d).start())
-    scattered[me] = partial[pl.ds(pl.multiple_of(me * 16, 16), 16), :]
+    scattered[me] = partial[pl.ds(pl.multiple_of(me * 8, 8), 8), :]
     each(1, 8, rs_arrived)
     shared[fib] = jnp.sum(scattered[...], axis=0)
     each(1, 16, lambda d: ar_copy(d).start())
     each(1, 16, ar_arrived)
-    reduced[pl.ds(pl.multiple_of(me * 16, 16), 16), :] = jnp.sum(shared[...], axis=0)
+    reduced[pl.ds(pl.multiple_of(me * 8, 8), 8), :] = jnp.sum(shared[...], axis=0)
     each(1, 8, lambda d: ag_copy(d).start())
     each(1, 8, ag_arrived)
-    target[...] = reduced[...]
+
+    updated[...] = reduced[...]
+
+    def cholesky_qr(repeat):
+        rows = updated[...]
+        crossed = lax.dot_general(rows, rows, (((1,), (1,)), ((), ())), precision=HIGHEST, preferred_element_type=F32)
+        updated[...] = jnp.dot(eliminate(crossed), rows, precision=HIGHEST, preferred_element_type=F32)
+
+    each(0, 2, cholesky_qr)
+    one_stack[...] = halves(updated[...])
+
+    def core(step):
+        both = dot(one_stack[...], fibers_high[step])
+        out = both[:64] + both[64:] + dot(one_stack[:64, :], fibers_low[step])
+        across = jnp.concatenate([out[:, :128], out[:, 128:]], axis=0).T
+        for half in range(2):
+            for peer in range(8):
+                start = half * 64 + peer * 8
+                core_out[peer, pl.ds(pl.multiple_of(step * 16 + half * 8, 8), 8), :] = across[start : start + 8, :]
+
+    each(0, 8, core)
+
+    def core_copy(d):
+        device, peer = plane_peer(d)
+        return remote(core_out.at[peer], core_in.at[me], core_send.at[d], core_recv.at[me], device)
+
+    def core_arrived(d):
+        device, peer = plane_peer(d)
+        remote(core_in.at[peer], core_in.at[peer], core_send.at[d], core_recv.at[peer], device).wait_recv()
+
+    each(1, 8, lambda d: core_copy(d).start())
+    core_in[me] = core_out[me]
+    each(1, 8, core_arrived)
+    collected[...] = core_in[...]
+
+    each(1, 8, lambda d: core_copy(d).wait_send())
 
     each(1, 8, lambda d: rs_copy(d).wait_send())
     each(1, 16, lambda d: ar_copy(d).wait_send())
@@ -336,60 +370,6 @@
     each(1, 4, lambda s: two_copy(s, row).wait_send())
     three_copy().wait_send()
     each(0, CHUNKS, lambda chunk: each(1, 16, lambda d: f_copy(chunk, d).wait_send()))
-    out_copy.wait()
-
-
-def core_kernel(updated, fibers, gathered, stacked, outgoing, incoming, send, recv):
-    fib, row, slab = place()
-    me = row * 2 + slab
-    stacked[...] = stack(updated[...])
-    greet(True, False)
-
-    def project(group):
-        folded = []
-        for s in range(4):
-            high, low = split(rows_of(fibers, group * 4 + s))
-            out = dot(stacked[...], jnp.concatenate([high, low], axis=0))
-            folded.append(fold(out[:256] + out[256:]))
-        left = left_half((64, 128))
-        square = jnp.concatenate(
-            [jnp.where(left, folded[0], folded[1]), jnp.where(left, folded[2], folded[3])], axis=0
-        )
-        turned = square.T
-        for half in range(2):
-            for peer in range(8):
-                start = half * 64 + peer * 8
-                at = pl.ds(pl.multiple_of(group * 16 + half * 8, 8), 8)
-                outgoing[peer, at, :] = turned[start : start + 8, :]
-
-    each(0, 8, project)
-
-    def copy(d):
-        device, peer = plane_peer(d)
-        return remote(outgoing.at[peer], incoming.at[me], send.at[d], recv.at[me], device)
-
-    def arrived(d):
-        device, peer = plane_peer(d)
-        remote(incoming.at[peer], incoming.at[peer], send.at[d], recv.at[peer], device).wait_recv()
-
-    each(1, 8, lambda d: copy(d).start())
-    incoming[me] = outgoing[me]
-    each(1, 8, arrived)
-    gathered[...] = incoming[...]
-    each(1, 8, lambda d: copy(d).wait_send())
-
-
-def turned(matrix):
-    return matrix.reshape(128, 4, 64).transpose(1, 2, 0).reshape(256, 128)
-
-
-def orthonormal(target):
-    result = target
-    for repeat in range(2):
-        crossed = jnp.dot(result.T, result, precision=HIGHEST)
-        cholesky_factor = jnp.linalg.cholesky(crossed)
-        result = jax.scipy.linalg.solve_triangular(cholesky_factor, result.T, lower=True).T
-    return result
 
 
 def body(tensor, factor_one, factor_two, factor_three, factor_four):
@@ -402,47 +382,40 @@
     vmem = pl.BlockSpec(memory_space=pltpu.VMEM)
     hbm = pl.BlockSpec(memory_space=pl.ANY)
     dma = pltpu.SemaphoreType.DMA
-    target, fibers = pl.pallas_call(
-        project_kernel,
-        out_shape=(jax.ShapeDtypeStruct((128, 256), F32), jax.ShapeDtypeStruct((2, 4096, 128), F32)),
+    updated, core = pl.pallas_call(
+        kernel,
+        out_shape=(jax.ShapeDtypeStruct((64, 512), F32), jax.ShapeDtypeStruct((8, 128, 128), F32)),
         in_specs=[hbm, vmem, vmem, vmem, vmem],
-        out_specs=(vmem, hbm),
+        out_specs=(vmem, vmem),
         scratch_shapes=[
             pltpu.VMEM((128, 256), BF16),
-            pltpu.VMEM((512, 256), BF16),
+            pltpu.VMEM((128, 512), BF16),
             pltpu.VMEM((3, 4096, 128), F32),
             pltpu.VMEM((CHUNKS, 2048, 128), F32),
             pltpu.VMEM((CHUNKS, 2048, 128), F32),
             pltpu.VMEM((4, 512, 128), F32),
-            pltpu.VMEM((CHUNKS, 2, 512, 128), F32),
-            pltpu.VMEM((2, 4096, 128), F32),
+            pltpu.VMEM((CHUNKS, 1024, 128), F32),
+            pltpu.VMEM((8192, 128), F32),
             pltpu.VMEM((4, 32, 128), F32),
             pltpu.VMEM((2, 64, 256), F32),
             pltpu.VMEM((4, 128, 256), BF16),
             pltpu.VMEM((4, 128, 256), BF16),
-            pltpu.VMEM((32, 64, 128), F32),
-            pltpu.VMEM((128, 256), F32),
-            pltpu.VMEM((8, 16, 256), F32),
-            pltpu.VMEM((16, 16, 256), F32),
-            pltpu.VMEM((128, 256), F32),
+            pltpu.VMEM((8, 512, 256), BF16),
+            pltpu.VMEM((8, 512, 256), BF16),
+            pltpu.VMEM((64, 512), F32),
+            pltpu.VMEM((8, 8, 512), F32),
+            pltpu.VMEM((16, 8, 512), F32),
+            pltpu.VMEM((64, 512), F32),
+            pltpu.VMEM((8, 128, 128), F32),
+            pltpu.VMEM((8, 128, 128), F32),
             dma((3,)), dma((CHUNKS,)), dma((CHUNKS, 8)), dma((CHUNKS, 8)), dma((CHUNKS,)), dma((CHUNKS, 16)), dma((CHUNKS, 16)),
-            dma((4,)), dma((4,)), dma(()), dma(()), dma((2,)), dma((8,)), dma((8,)), dma((16,)), dma((16,)), dma((8,)), dma((8,)), dma(()),
+            dma((4,)), dma((4,)), dma(()), dma(()), dma((2,)), dma((8,)), dma((8,)), dma((16,)), dma((16,)), dma((8,)), dma((8,)), dma((8,)), dma((8,)),
         ],
-        compiler_params=pltpu.CompilerParams(collective_id=0, has_side_effects=True, vmem_limit_bytes=52 * 2**20),
-        name="project",
-    )(tensor.reshape(8, 4096, 128), factor_four.T, three, two, turned(factor_one))
-    updated = orthonormal(target.reshape(512, 64))
-    core = pl.pallas_call(
-        core_kernel,
-        out_shape=jax.ShapeDtypeStruct((8, 128, 128), F32),
-        in_specs=[vmem, vmem],
-        out_specs=vmem,
-        scratch_shapes=[pltpu.VMEM((512, 256), BF16), pltpu.VMEM((8, 128, 128), F32), pltpu.VMEM((8, 128, 128), F32), dma((8,)), dma((8,))],
-        compiler_params=pltpu.CompilerParams(collective_id=1, has_side_effects=True, vmem_limit_bytes=32 * 2**20),
-        name="core",
-    )(turned(updated), fibers)
-    core = core.reshape(8, 4, 2, 2, 8, 2, 64).transpose(6, 4, 1, 0, 2, 5, 3).reshape(64, 8, 4, 64)
-    return (updated, core)
+        compiler_params=pltpu.CompilerParams(collective_id=0, has_side_effects=True, vmem_limit_bytes=56 * 2**20),
+        name="hooi",
+    )(tensor.reshape(8, 4096, 128), factor_four.T, three, two, factor_one.T)
+    core = core.reshape(8, 2, 4, 2, 8, 2, 64).transpose(6, 4, 3, 1, 0, 2, 5).reshape(64, 8, 4, 64)
+    return (updated.T, core)
 
 
 def solution(mesh):

time: 214 us -> 177 us (0.83)
  other arithmetic: 25.2 us -> 2.29 us
  Pallas kernels: 178 us -> 168 us
    another operation x10 -> x0, other arithmetic: 24.1 us -> none  [the longest x6 13 us: orthonormal(): cholesky_factor = jnp.linalg.cholesky(crossed)]
    pallas_call x2 -> x1, Pallas kernels: 178 us -> 168 us  [body(): pl.pallas_call(kernel, out_shape=(jax.ShapeDtypeStruct((64, 512), F32), j...]
    unnamed x9 -> x3, local copies, waits for them, and re-layouts: 6.66 us -> 4.24 us
where the time goes in v3:
time: 177 us
  Pallas kernels  168 us (95%)
  local copies, waits for them, and re-layouts  6.02 us (3%)
  other arithmetic  2.29 us (1%)
    pallas_call x1, Pallas kernels, body(): pl.pallas_call(kernel, out_shape=(jax.ShapeDtypeStruct((64, 512), F32), j...  168 us
    unnamed x3, local copies, waits for them, and re-layouts  4.24 us

profile of v3, /device:TPU:1, one launch (start us, length us, event | category | flops | bytes accessed | tf_op | source)
XLA Modules:
  0.0 176.7 jit_solution(17173702872218817194)
XLA Ops:
  0.6 1.5 pad_maximum_fusion.1.two
  2.1 0.8 copy.9
  2.9 0.1 pad_select_fusion
  3.0 0.7 pad_maximum_fusion.three
  3.7 167.7 %hooi.1 = (f32[64,512]{1,0:T(8,128)}, f32[8,128,128]{2,1,0:T(8,128)}) custom-call(f32[8,4096,128]{2,1,0:T(8,128)} %bitcast.8, f32[64,128]{1,0:T(8,128)} %bitcast.13, f32[64,256]{1,0:T(8,128)} %pad_maximum_fusion.three, f32[32,128]{1,0:T(8,128)} %pad_maximum_fusion.1.two, f32[64,512]{1,0:T(8,128)} %bitcast.10), custom_call_target="tpu_custom_call" | custom-call | tf_op jit(solution)/shard_map/hooi/pallas_call | solution.py:385
  171.4 1.7 reshape.14
  173.1 0.1 copy.10
  173.2 1.9 %copy.11 = f32[64,8,4,64]{3,2,1,0:T(4,128)} copy(f32[64,8,4,64]{0,1,3,2:T(8,128)S(1)} %bitcast.9) | data formatting | bytes 1048576
  175.1 1.6 copy.13

commit v4 on v3

v4 whole, which is shorter than its diff:
```python
import jax
import jax.numpy as jnp
from jax import lax
from jax.experimental import pallas as pl
from jax.experimental.pallas import tpu as pltpu
from jax.sharding import PartitionSpec as P

HIGHEST = lax.Precision.HIGHEST
MESH = pl.DeviceIdType.MESH
F32 = jnp.float32
BF16 = jnp.bfloat16
CHUNKS = 8
LAG = 2
PLANE = tuple(range(1, 8))
FIBERS = tuple(sorted(range(1, 16), key=lambda d: -(min(d // 4, 4 - d // 4) + min(d % 4, 4 - d % 4))))


def split(x):
    high = x.astype(BF16)
    return high, (x - high.astype(F32)).astype(BF16)


def dot(a, b):
    return jnp.dot(a, b, preferred_element_type=F32)


def dot_nt(a, b):
    return lax.dot_general(a, b, (((1,), (1,)), ((), ())), preferred_element_type=F32)


def place():
    return lax.axis_index("fib"), lax.axis_index("row"), lax.axis_index("slab")


def plane_peer(d):
    fib, row, slab = place()
    row, slab = lax.rem(row + d // 2, 4), lax.rem(slab + d % 2, 2)
    return (fib, row, slab), row * 2 + slab


def fib_peer(d):
    fib, row, slab = place()
    fib = lax.rem(fib // 4 + d // 4, 4) * 4 + lax.rem(fib % 4 + d % 4, 4)
    return (fib, row, slab), fib


def each(lower, upper, step, unroll=1):
    def run(index, carry):
        step(index)
        return carry

    lax.fori_loop(lower, upper, run, 0, unroll=unroll)


def remote(src, dst, send, recv, device):
    return pltpu.make_async_remote_copy(
        src_ref=src, dst_ref=dst, send_sem=send, recv_sem=recv, device_id=device, device_id_type=MESH
    )


def greet():
    barrier = pltpu.get_barrier_semaphore()
    for d in PLANE:
        pl.semaphore_signal(barrier, inc=1, device_id=plane_peer(d)[0], device_id_type=MESH)
    for d in FIBERS:
        pl.semaphore_signal(barrier, inc=1, device_id=fib_peer(d)[0], device_id_type=MESH)


def stack(x):
    high, low = split(x)
    return jnp.concatenate([jnp.concatenate([high, high], 1), jnp.concatenate([low, low], 1)], 0)


def left_half(shape):
    return lax.broadcasted_iota(jnp.int32, shape, 1) < 64


def halves(x):
    return jnp.concatenate(split(x), axis=0)


def eliminate(crossed, group=4):
    lane = lax.broadcasted_iota(jnp.int32, (8, 64), 1)
    row = lax.broadcasted_iota(jnp.int32, (8, 64), 0)
    below = lax.broadcasted_iota(jnp.int32, (8, 128), 0)
    blocks = [
        jnp.concatenate([crossed[8 * b : 8 * b + 8], jnp.where(lane == row + 8 * b, 1.0, 0.0)], axis=1) for b in range(8)
    ]

    def spread(x):
        return jnp.broadcast_to(x, (8, 128))

    for first in range(0, 64, group):
        b, k = first // 8, first % 8
        here = blocks[b]
        corner = [[spread(here[k + m : k + m + 1, first + n : first + n + 1]) for n in range(m + 1)] for m in range(group)]
        below_diagonal = [[None] * group for m in range(group)]
        scale = [None] * group
        for m in range(group):
            square = corner[m][m]
            for n in range(m):
                square = square - below_diagonal[m][n] * below_diagonal[m][n]
            scale[m] = lax.rsqrt(square)
            for other in range(m + 1, group):
                entry = corner[other][m]
                for n in range(m):
                    entry = entry - below_diagonal[other][n] * below_diagonal[m][n]
                below_diagonal[other][m] = entry * scale[m]

        def forward(parts):
            done = []
            for m in range(group):
                part = parts[m]
                for n in range(m):
                    part = part - done[n] * below_diagonal[m][n]
                done.append(part * scale[m])
            return done

        pivots = forward([spread(here[k + m : k + m + 1, :]) for m in range(group)])
        for at in range(b, 8):
            if at == b and k + group == 8:
                update = here
            else:
                columns = forward([spread(blocks[at][:, first + m : first + m + 1]) for m in range(group)])
                update = blocks[at]
                for m in range(group):
                    update = update - columns[m] * pivots[m]
            if at == b:
                update = jnp.where(below < k, here, update)
                for m in range(group):
                    update = jnp.where(below == k + m, pivots[m], update)
            blocks[at] = update
    return jnp.concatenate(blocks, axis=0)[:, 64:]


def kernel(
    tensor, four, three, two, one, updated, collected, four_stack, one_stack, three_own_block, two_own_block,
    staged, outgoing, incoming, halfway, contracted, fibers, two_all, three_all, three_stack, wide_high, wide_low,
    fibers_high, fibers_low, partial, scattered, shared, reduced, core_out, core_in,
    load_sem, own_sem, z_send, z_recv, fib_own_sem, f_send, f_recv,
    two_send, two_recv, three_send, three_recv, rs_send, rs_recv, ar_send, ar_recv, ag_send, ag_recv, core_send, core_recv,
):
    fib, row, slab = place()
    me = row * 2 + slab

    def load(chunk):
        return pltpu.make_async_copy(tensor.at[chunk], staged.at[chunk % 3], load_sem.at[chunk % 3])

    def mode_four(chunk):
        slot = chunk % 3

        def two_steps(pair):
            first = staged[slot, pl.ds(2 * pair, 128, stride=32), :]
            second = staged[slot, pl.ds(2 * pair + 1, 128, stride=32), :]
            high, low = split(jnp.concatenate([first, second], axis=0))
            out = dot_nt(four_stack[...], jnp.concatenate([high, low], axis=1))
            out = out[:64] + out[64:]
            outgoing[chunk, pl.ds(2 * pair, 64, stride=32), :] = out[:, :128]
            outgoing[chunk, pl.ds(2 * pair + 1, 64, stride=32), :] = out[:, 128:]

        each(0, 16, two_steps, unroll=2)

    load(0).start()
    load(1).start()
    greet()
    four_stack[...] = stack(four[...].T)
    load(0).wait()
    load(2).start()
    mode_four(0)
    pl.semaphore_wait(pltpu.get_barrier_semaphore(), len(PLANE) + len(FIBERS))

    def z_copy(chunk, half, d):
        device, peer = plane_peer(d)
        return remote(
            outgoing.at[chunk, pl.ds(peer * 256 + half * 128, 128), :],
            incoming.at[chunk, half, pl.ds(me * 128, 128), :],
            z_send.at[chunk, half], z_recv.at[chunk, half], device,
        )

    def z_all(chunk, half):
        block = incoming.at[chunk, half, pl.ds(0, 7 * 128), :]
        return remote(block, block, z_send.at[chunk, half], z_recv.at[chunk, half], plane_peer(1)[0])

    def z_own(chunk, half):
        return pltpu.make_async_copy(
            outgoing.at[chunk, pl.ds(me * 256 + half * 128, 128), :],
            incoming.at[chunk, half, pl.ds(me * 128, 128), :],
            own_sem.at[chunk, half],
        )

    def send_chunk(chunk):
        for half in range(2):
            for d in PLANE:
                z_copy(chunk, half, d).start()
            z_own(chunk, half).start()

    def sent_chunk(chunk):
        for half in range(2):
            z_all(chunk, half).wait_send()

    def f_rows(chunk, half, device):
        return fibers.at[pl.ds((device * CHUNKS + chunk) * 4, 4), half]

    def f_copy(chunk, half, d):
        device, peer = fib_peer(d)
        return remote(contracted.at[chunk, half, peer], f_rows(chunk, half, fib), f_send, f_recv, device)

    def f_all():
        block = fibers.at[pl.ds(0, 15 * CHUNKS * 4)]
        return remote(block, block, f_send, f_recv, fib_peer(1)[0])

    def f_own(chunk, half):
        return pltpu.make_async_copy(contracted.at[chunk, half, fib], f_rows(chunk, half, fib), fib_own_sem.at[chunk, half])

    def two_copy(step):
        return remote(two_own_block, two_all.at[row], two_send, two_recv, (fib, lax.rem(row + step, 4), slab))

    def two_arrived():
        block = two_all.at[pl.ds(0, 3)]
        return remote(block, block, two_send, two_recv, (fib, lax.rem(row + 1, 4), slab))

    def three_copy():
        return remote(three_own_block, three_all.at[slab], three_send, three_recv, (fib, row, 1 - slab))

    def exchange_factors():
        two_own_block[...] = jnp.concatenate([two[...], two[...]], axis=1)
        across = three[...].T
        nothing = jnp.zeros_like(across)
        mine = jnp.where(slab == 0, 1.0, 0.0)
        block = jnp.concatenate([across * mine, across * (1.0 - mine)], axis=1)
        three_own_block[...] = jnp.concatenate([block] * 4, axis=1)
        for step in range(1, 4):
            two_copy(step).start()
        three_copy().start()
        two_all[row] = two_own_block[...]
        three_all[slab] = three_own_block[...]

    def widen():
        two_arrived().wait_recv()
        three_copy().wait_recv()
        high, low = split(three_all[0] + three_all[1])
        lanes = lax.broadcasted_iota(jnp.int32, (64, 256), 1)
        three_stack[...] = jnp.where(lanes < 128, high.astype(F32), low.astype(F32)).astype(BF16)
        left = left_half((32, 128))
        nothing = jnp.zeros((32, 128), F32)
        for z in range(4):
            block = two_all[z]
            sides = (jnp.where(left, block, 0.0), jnp.where(left, 0.0, block))
            pieces = []
            for i in range(4):
                tiles = [nothing, nothing]
                tiles[i // 2] = sides[i % 2]
                pieces.append(jnp.concatenate(tiles, axis=1))
            high, low = split(jnp.concatenate(pieces, axis=0))
            wide_high[z] = high
            wide_low[z] = low
        one_stack[...] = halves(one[...].T)

    def modes_three_two(chunk, half):
        def rank(r):
            parts = []
            for z in range(4):
                pieces = [incoming[chunk, half, pl.ds((2 * z + c) * 128 + r * 32, 32), :] for c in range(2)]
                high, low = split(jnp.concatenate(pieces, axis=0))
                parts.append(jnp.concatenate([high, low, high, low], axis=0))
            out = dot(three_stack[...], jnp.concatenate(parts, axis=1))
            for z in range(4):
                halfway[z, pl.ds(r, 64, stride=4), :] = out[:, z * 128 : (z + 1) * 128]

        each(0, 4, rank, unroll=2)

        def rows(block):
            at = pl.ds(pl.multiple_of(block * 128, 128), 128)
            total = jnp.zeros((128, 256), F32)
            for z in range(4):
                high, low = split(halfway[z, at, :])
                both = dot(jnp.concatenate([high, low], axis=0), wide_high[z])
                total = total + both[:128] + both[128:] + dot(high, wide_low[z])
            left = left_half((8, 128))
            for f in range(8):
                for t in range(2):
                    lower = total[f * 16 : f * 16 + 8, t * 128 : t * 128 + 128]
                    upper = total[f * 16 + 8 : f * 16 + 16, t * 128 : t * 128 + 128]
                    contracted[chunk, half, block * 8 + f, 2 * t] = jnp.where(left, lower, pltpu.roll(upper, 64, 1))
                    contracted[chunk, half, block * 8 + f, 2 * t + 1] = jnp.where(left, pltpu.roll(lower, 64, 1), upper)

        each(0, 2, rows)

    def advance(turn):
        @pl.when(turn < CHUNKS)
        def _():
            @pl.when(turn >= 2)
            def _():
                sent_chunk(turn - 2)

            send_chunk(turn)

        @pl.when(turn == 0)
        def _():
            exchange_factors()

        @pl.when(turn + 1 < CHUNKS)
        def _():
            load(turn + 1).wait()

            @pl.when(turn + 3 < CHUNKS)
            def _():
                load(turn + 3).start()

            mode_four(turn + 1)

        @pl.when(turn == 0)
        def _():
            widen()

        @pl.when(turn >= LAG)
        def _():
            chunk = turn - LAG

            def one_half(half):
                z_own(chunk, half).wait()
                z_all(chunk, half).wait_recv()
                modes_three_two(chunk, half)
                for d in FIBERS:
                    f_copy(chunk, half, d).start()
                f_own(chunk, half).start()

            each(0, 2, one_half)

    each(0, CHUNKS + LAG, advance)
    each(CHUNKS - 2, CHUNKS, sent_chunk)
    partial[...] = jnp.zeros_like(partial)
    each(0, CHUNKS, lambda chunk: each(0, 2, lambda half: f_own(chunk, half).wait()))
    f_all().wait_recv()
    fiber_rows = fibers.reshape(8192, 128)

    def cross(step):
        block = jnp.concatenate([fiber_rows[pl.ds(2 * step + n, 512, stride=16), :] for n in range(2)], axis=1)
        high, low = split(block)
        fibers_high[step] = high
        fibers_low[step] = low
        both = dot(one_stack[...], high)
        both_parts = halves(both[:64] + both[64:] + dot(one_stack[:64, :], low))
        back = dot_nt(both_parts, high)
        partial[...] += back[:64] + back[64:] + dot_nt(both_parts[:64], low)

    each(0, 8, cross, unroll=2)

    def rs_copy(d):
        device, peer = plane_peer(d)
        return remote(partial.at[pl.ds(peer * 8, 8), :], scattered.at[me], rs_send, rs_recv, device)

    def ar_copy(d):
        return remote(shared.at[fib], shared.at[fib], ar_send, ar_recv, fib_peer(d)[0])

    def ag_copy(d):
        mine = reduced.at[pl.ds(me * 8, 8), :]
        return remote(mine, mine, ag_send, ag_recv, plane_peer(d)[0])

    def rs_all():
        block = scattered.at[pl.ds(0, 7)]
        return remote(block, block, rs_send, rs_recv, plane_peer(1)[0])

    def ar_all():
        block = shared.at[pl.ds(0, 15)]
        return remote(block, block, ar_send, ar_recv, fib_peer(1)[0])

    def ag_all():
        block = reduced.at[pl.ds(0, 56), :]
        return remote(block, block, ag_send, ag_recv, plane_peer(1)[0])

    for d in PLANE:
        rs_copy(d).start()
    scattered[me] = partial[pl.ds(pl.multiple_of(me * 8, 8), 8), :]
    rs_all().wait_recv()
    shared[fib] = jnp.sum(scattered[...], axis=0)
    for d in FIBERS:
        ar_copy(d).start()
    ar_all().wait_recv()
    reduced[pl.ds(pl.multiple_of(me * 8, 8), 8), :] = jnp.sum(shared[...], axis=0)
    for d in PLANE:
        ag_copy(d).start()
    ag_all().wait_recv()

    updated[...] = reduced[...]

    def cholesky_qr(repeat):
        rows = updated[...]
        crossed = lax.dot_general(rows, rows, (((1,), (1,)), ((), ())), precision=HIGHEST, preferred_element_type=F32)
        updated[...] = jnp.dot(eliminate(crossed), rows, precision=HIGHEST, preferred_element_type=F32)

    each(0, 2, cholesky_qr)
    one_stack[...] = halves(updated[...])

    def core(step):
        both = dot(one_stack[...], fibers_high[step])
        out = both[:64] + both[64:] + dot(one_stack[:64, :], fibers_low[step])
        across = jnp.concatenate([out[:, :128], out[:, 128:]], axis=0).T
        for half in range(2):
            for peer in range(8):
                start = half * 64 + peer * 8
                core_out[peer, pl.ds(pl.multiple_of(step * 16 + half * 8, 8), 8), :] = across[start : start + 8, :]

    each(0, 8, core, unroll=2)

    def core_copy(d):
        device, peer = plane_peer(d)
        return remote(core_out.at[peer], core_in.at[me], core_send, core_recv, device)

    def core_all():
        block = core_in.at[pl.ds(0, 7)]
        return remote(block, block, core_send, core_recv, plane_peer(1)[0])

    for d in PLANE:
        core_copy(d).start()
    core_in[me] = core_out[me]
    core_all().wait_recv()
    collected[...] = core_in[...]

    core_all().wait_send()
    rs_all().wait_send()
    ar_all().wait_send()
    ag_all().wait_send()
    two_arrived().wait_send()
    three_copy().wait_send()
    f_all().wait_send()


def body(tensor, factor_one, factor_two, factor_three, factor_four):
    vmem = pl.BlockSpec(memory_space=pltpu.VMEM)
    hbm = pl.BlockSpec(memory_space=pl.ANY)
    dma = pltpu.SemaphoreType.DMA
    updated, core = pl.pallas_call(
        kernel,
        out_shape=(jax.ShapeDtypeStruct((64, 512), F32), jax.ShapeDtypeStruct((8, 128, 128), F32)),
        in_specs=[hbm, vmem, vmem, vmem, vmem],
        out_specs=(vmem, vmem),
        scratch_shapes=[
            pltpu.VMEM((128, 256), BF16),
            pltpu.VMEM((128, 512), BF16),
            pltpu.VMEM((64, 256), F32),
            pltpu.VMEM((32, 128), F32),
            pltpu.VMEM((3, 4096, 128), F32),
            pltpu.VMEM((CHUNKS, 2048, 128), F32),
            pltpu.VMEM((CHUNKS, 2, 1024, 128), F32),
            pltpu.VMEM((4, 256, 128), F32),
            pltpu.VMEM((CHUNKS, 2, 16, 4, 8, 128), F32),
            pltpu.VMEM((512, 2, 8, 128), F32),
            pltpu.VMEM((4, 32, 128), F32),
            pltpu.VMEM((2, 64, 256), F32),
            pltpu.VMEM((64, 256), BF16),
            pltpu.VMEM((4, 128, 256), BF16),
            pltpu.VMEM((4, 128, 256), BF16),
            pltpu.VMEM((8, 512, 256), BF16),
            pltpu.VMEM((8, 512, 256), BF16),
            pltpu.VMEM((64, 512), F32),
            pltpu.VMEM((8, 8, 512), F32),
            pltpu.VMEM((16, 8, 512), F32),
            pltpu.VMEM((64, 512), F32),
            pltpu.VMEM((8, 128, 128), F32),
            pltpu.VMEM((8, 128, 128), F32),
            dma((3,)), dma((CHUNKS, 2)), dma((CHUNKS, 2)), dma((CHUNKS, 2)), dma((CHUNKS, 2)), dma(()), dma(()),
            dma(()), dma(()), dma(()), dma(()), dma(()), dma(()), dma(()), dma(()), dma(()), dma(()), dma(()), dma(()),
        ],
        compiler_params=pltpu.CompilerParams(collective_id=0, has_side_effects=True, vmem_limit_bytes=56 * 2**20),
        name="hooi",
    )(tensor.reshape(8, 4096, 128), factor_four, factor_three, factor_two, factor_one)
    core = core.reshape(8, 2, 2, 2, 2, 8, 2, 64).transpose(7, 5, 4, 2, 0, 1, 3, 6).reshape(64, 8, 4, 64)
    return (updated.T, core)


def solution(mesh):
    in_specs = (P("fib", "row", "slab", None), P(), P("row", None), P("slab", None), P())
    out_specs = (P(), P(None, ("row", "slab"), "fib", None))
    return jax.shard_map(body, mesh=mesh, in_specs=in_specs, out_specs=out_specs, check_vma=False)
```

time: 177 us -> 158 us (0.89)
  Pallas kernels: 168 us -> 149 us
  local copies, waits for them, and re-layouts: 6.02 us -> 8.46 us
  other arithmetic: 2.29 us -> 0 us
    pallas_call x1, Pallas kernels: 168 us -> 149 us  [body(): pl.pallas_call(kernel, out_shape=(jax.ShapeDtypeStruct((64, 512), F32), j...]
    unnamed x3 -> x4, local copies, waits for them, and re-layouts: 4.24 us -> 6.67 us
    concatenate x2 -> x0, other arithmetic: 2.21 us -> none  [the longest x1 1.47 us: body(): two = jnp.concatenate([factor_two, factor_two], 1)]
where the time goes in v4:
time: 158 us
  Pallas kernels  149 us (94%)
  local copies, waits for them, and re-layouts  8.46 us (5%)
    pallas_call x1, Pallas kernels, body(): pl.pallas_call(kernel, out_shape=(jax.ShapeDtypeStruct((64, 512), F32), j...  149 us
    unnamed x4, local copies, waits for them, and re-layouts  6.67 us

profile of v4, /device:TPU:1, one launch (start us, length us, event | category | flops | bytes accessed | tf_op | source)
XLA Modules:
  0.0 158.0 jit_solution(9025748825272730445)
XLA Ops:
  0.6 1.5 copy.10.four
  2.1 1.7 %copy.11.one = f32[512,64]{1,0:T(8,128)} copy(f32[512,64]{0,1:T(8,128)} %param.6) | data formatting | bytes 262144 | tf_op args[1]
  3.9 148.9 %hooi.1 = (f32[64,512]{1,0:T(8,128)}, f32[8,128,128]{2,1,0:T(8,128)}) custom-call(f32[8,4096,128]{2,1,0:T(8,128)} %bitcast.5, f32[128,64]{1,0:T(8,128)} %copy.10.four, f32[32,64]{1,0:T(8,128)} %three.1, f32[32,64]{1,0:T(8,128)} %two.1, f32[512,64]{1,0:T(8,128)} %copy.11.one), custom_call_target="tpu_custom_call" | custom-call | tf_op jit(solution)/shard_map/hooi/pallas_call | solution.py:433
  152.7 1.7 %reshape.14 = f32[8,2,2,2,2,8,2,64]{7,6,5,4,3,2,1,0:T(2,128)S(1)} reshape(f32[8,128,128]{2,1,0:T(8,128)} %get-tuple-element.5) | data formatting | bytes 1048576 | tf_op jit(solution)/shard_map/reshape | solution.py:468
  154.4 0.1 copy.12
  154.5 1.9 %copy.13 = f32[64,8,4,64]{3,2,1,0:T(4,128)} copy(f32[64,8,4,64]{0,1,3,2:T(8,128)S(1)} %bitcast.6) | data formatting | bytes 1048576
  156.4 1.6 copy.15

commit v5 on v4

--- a/solution.py
+++ b/solution.py
@@ -134,10 +134,11 @@
 
 
 def kernel(
-    tensor, four, three, two, one, updated, collected, four_stack, one_stack, three_own_block, two_own_block,
+    tensor, four_hbm, three_hbm, two_hbm, one_hbm, updated, collected,
+    four, three, two, one, dealt, four_stack, one_stack, three_own_block, two_own_block,
     staged, outgoing, incoming, halfway, contracted, fibers, two_all, three_all, three_stack, wide_high, wide_low,
-    fibers_high, fibers_low, partial, scattered, shared, reduced, core_out, core_in,
-    load_sem, own_sem, z_send, z_recv, fib_own_sem, f_send, f_recv,
+    fibers_high, fibers_low, partial, scattered, shared, state, core_out, core_in,
+    load_sem, factor_sem, own_sem, z_send, z_recv, fib_own_sem, f_send, f_recv,
     two_send, two_recv, three_send, three_recv, rs_send, rs_recv, ar_send, ar_recv, ag_send, ag_recv, core_send, core_recv,
 ):
     fib, row, slab = place()
@@ -160,10 +161,21 @@
 
         each(0, 16, two_steps, unroll=2)
 
+    def fetch(n):
+        source, target = ((four_hbm, four), (three_hbm, three), (two_hbm, two), (one_hbm, one))[n]
+        return pltpu.make_async_copy(source, target, factor_sem.at[n])
+
+    fetch(0).start()
     load(0).start()
     load(1).start()
+    for n in range(1, 4):
+        fetch(n).start()
     greet()
-    four_stack[...] = stack(four[...].T)
+    fetch(0).wait()
+    across = four[...]
+    dealt[pl.ds(0, 32, stride=2), :] = across[:32]
+    dealt[pl.ds(1, 32, stride=2), :] = across[32:]
+    four_stack[...] = stack(dealt[...])
     load(0).wait()
     load(2).start()
     mode_four(0)
@@ -223,6 +235,8 @@
         return remote(three_own_block, three_all.at[slab], three_send, three_recv, (fib, row, 1 - slab))
 
     def exchange_factors():
+        fetch(1).wait()
+        fetch(2).wait()
         two_own_block[...] = jnp.concatenate([two[...], two[...]], axis=1)
         across = three[...].T
         nothing = jnp.zeros_like(across)
@@ -254,7 +268,8 @@
             high, low = split(jnp.concatenate(pieces, axis=0))
             wide_high[z] = high
             wide_low[z] = low
-        one_stack[...] = halves(one[...].T)
+        fetch(3).wait()
+        one_stack[...] = halves(one[...])
 
     def modes_three_two(chunk, half):
         def rank(r):
@@ -354,7 +369,7 @@
         return remote(shared.at[fib], shared.at[fib], ar_send, ar_recv, fib_peer(d)[0])
 
     def ag_copy(d):
-        mine = reduced.at[pl.ds(me * 8, 8), :]
+        mine = state.at[pl.ds(me * 8, 8), pl.ds(0, 512)]
         return remote(mine, mine, ag_send, ag_recv, plane_peer(d)[0])
 
     def rs_all():
@@ -366,7 +381,7 @@
         return remote(block, block, ar_send, ar_recv, fib_peer(1)[0])
 
     def ag_all():
-        block = reduced.at[pl.ds(0, 56), :]
+        block = state.at[pl.ds(0, 56), pl.ds(0, 512)]
         return remote(block, block, ag_send, ag_recv, plane_peer(1)[0])
 
     for d in PLANE:
@@ -377,50 +392,78 @@
     for d in FIBERS:
         ar_copy(d).start()
     ar_all().wait_recv()
-    reduced[pl.ds(pl.multiple_of(me * 8, 8), 8), :] = jnp.sum(shared[...], axis=0)
+    state[pl.ds(pl.multiple_of(me * 8, 8), 8), pl.ds(0, 512)] = jnp.sum(shared[...], axis=0)
     for d in PLANE:
         ag_copy(d).start()
     ag_all().wait_recv()
 
-    updated[...] = reduced[...]
-
-    def cholesky_qr(repeat):
-        rows = updated[...]
-        crossed = lax.dot_general(rows, rows, (((1,), (1,)), ((), ())), precision=HIGHEST, preferred_element_type=F32)
-        updated[...] = jnp.dot(eliminate(crossed), rows, precision=HIGHEST, preferred_element_type=F32)
-
-    each(0, 2, cholesky_qr)
-    one_stack[...] = halves(updated[...])
-
-    def core(step):
+    one_stack[...] = halves(state[:, :512])
+
+    def project(n):
+        p_low, middle = n // 4, n % 4
+        step = (middle // 2) * 4 + p_low * 2 + middle % 2
         both = dot(one_stack[...], fibers_high[step])
         out = both[:64] + both[64:] + dot(one_stack[:64, :], fibers_low[step])
         across = jnp.concatenate([out[:, :128], out[:, 128:]], axis=0).T
-        for half in range(2):
+        for high in range(2):
             for peer in range(8):
-                start = half * 64 + peer * 8
-                core_out[peer, pl.ds(pl.multiple_of(step * 16 + half * 8, 8), 8), :] = across[start : start + 8, :]
-
-    each(0, 8, core, unroll=2)
+                start = high * 64 + peer * 8
+                at = pl.ds(pl.multiple_of(middle * 16 + high * 8, 8), 8)
+                core_out[peer, p_low, at, :] = across[start : start + 8, :]
+
+    each(0, 8, project, unroll=2)
 
     def core_copy(d):
         device, peer = plane_peer(d)
-        return remote(core_out.at[peer], core_in.at[me], core_send, core_recv, device)
+        return remote(core_out.at[peer], core_in.at[:, me], core_send, core_recv, device)
 
     def core_all():
-        block = core_in.at[pl.ds(0, 7)]
+        block = core_in.at[:, pl.ds(0, 7)]
         return remote(block, block, core_send, core_recv, plane_peer(1)[0])
 
     for d in PLANE:
         core_copy(d).start()
-    core_in[me] = core_out[me]
+    for p_low in range(2):
+        core_in[p_low, me] = core_out[me, p_low]
+
+    ag_all().wait_send()
+    lanes = lax.broadcasted_iota(jnp.int32, (64, 128), 1)
+    state[:, 512:] = jnp.where(lanes == lax.broadcasted_iota(jnp.int32, (64, 128), 0), 1.0, 0.0)
+
+    def cholesky_qr(repeat):
+        rows = state[:, :512]
+        crossed = lax.dot_general(rows, rows, (((1,), (1,)), ((), ())), precision=HIGHEST, preferred_element_type=F32)
+        state[...] = jnp.dot(eliminate(crossed), state[...], precision=HIGHEST, preferred_element_type=F32)
+
+    each(0, 2, cholesky_qr)
+    updated[...] = state[:, :512]
+    inverse = state[:, 512:]
+    weights = halves(jnp.concatenate([inverse, pltpu.roll(inverse, 64, 1)], axis=0))
+
     core_all().wait_recv()
-    collected[...] = core_in[...]
+    core_rows = core_in.reshape(1024, 128)
+
+    def finish(n):
+        start = (n % 2) * 512 + (n // 2) * 8
+        block = jnp.concatenate([core_rows[pl.ds(start + q, 32, stride=16), :] for q in range(8)], axis=0)
+        high, low = split(block)
+        both = dot_nt(weights, high)
+        out = both[:128] + both[128:] + dot_nt(weights[:128], low)
+        for q in range(8):
+            tile, off = q // 4, (q % 4) * 32
+            lower = out[:64, tile * 128 : tile * 128 + 128]
+            upper = out[64:, tile * 128 : tile * 128 + 128]
+            if off:
+                lower = pltpu.roll(lower, 128 - off, 1)
+            if off != 32:
+                upper = pltpu.roll(upper, (160 - off) % 128, 1)
+            collected[pl.ds(q * 4 + n, 64, stride=32), :] = jnp.where(lanes < 32, lower, upper)
+
+    each(0, 4, finish)
 
     core_all().wait_send()
     rs_all().wait_send()
     ar_all().wait_send()
-    ag_all().wait_send()
     two_arrived().wait_send()
     three_copy().wait_send()
     f_all().wait_send()
@@ -432,10 +475,15 @@
     dma = pltpu.SemaphoreType.DMA
     updated, core = pl.pallas_call(
         kernel,
-        out_shape=(jax.ShapeDtypeStruct((64, 512), F32), jax.ShapeDtypeStruct((8, 128, 128), F32)),
-        in_specs=[hbm, vmem, vmem, vmem, vmem],
+        out_shape=(jax.ShapeDtypeStruct((64, 512), F32), jax.ShapeDtypeStruct((2048, 128), F32)),
+        in_specs=[hbm] * 5,
         out_specs=(vmem, vmem),
         scratch_shapes=[
+            pltpu.VMEM((64, 128), F32),
+            pltpu.VMEM((32, 64), F32),
+            pltpu.VMEM((32, 64), F32),
+            pltpu.VMEM((64, 512), F32),
+            pltpu.VMEM((64, 128), F32),
             pltpu.VMEM((128, 256), BF16),
             pltpu.VMEM((128, 512), BF16),
             pltpu.VMEM((64, 256), F32),
@@ -456,17 +504,16 @@
             pltpu.VMEM((64, 512), F32),
             pltpu.VMEM((8, 8, 512), F32),
             pltpu.VMEM((16, 8, 512), F32),
-            pltpu.VMEM((64, 512), F32),
-            pltpu.VMEM((8, 128, 128), F32),
-            pltpu.VMEM((8, 128, 128), F32),
-            dma((3,)), dma((CHUNKS, 2)), dma((CHUNKS, 2)), dma((CHUNKS, 2)), dma((CHUNKS, 2)), dma(()), dma(()),
+            pltpu.VMEM((64, 640), F32),
+            pltpu.VMEM((8, 2, 64, 128), F32),
+            pltpu.VMEM((2, 8, 64, 128), F32),
+            dma((3,)), dma((4,)), dma((CHUNKS, 2)), dma((CHUNKS, 2)), dma((CHUNKS, 2)), dma((CHUNKS, 2)), dma(()), dma(()),
             dma(()), dma(()), dma(()), dma(()), dma(()), dma(()), dma(()), dma(()), dma(()), dma(()), dma(()), dma(()),
         ],
         compiler_params=pltpu.CompilerParams(collective_id=0, has_side_effects=True, vmem_limit_bytes=56 * 2**20),
         name="hooi",
-    )(tensor.reshape(8, 4096, 128), factor_four, factor_three, factor_two, factor_one)
-    core = core.reshape(8, 2, 2, 2, 2, 8, 2, 64).transpose(7, 5, 4, 2, 0, 1, 3, 6).reshape(64, 8, 4, 64)
-    return (updated.T, core)
+    )(tensor.reshape(8, 4096, 128), factor_four.T, factor_three, factor_two, factor_one.T)
+    return (updated.T, core[:, :64].reshape(64, 8, 4, 64))
 
 
 def solution(mesh):

time: 158 us -> 148 us (0.937)
  Pallas kernels: 149 us -> 143 us
  local copies, waits for them, and re-layouts: 8.46 us -> 3.83 us
    pallas_call x1, Pallas kernels: 149 us -> 143 us  [body(): pl.pallas_call(kernel, out_shape=(jax.ShapeDtypeStruct((64, 512), F32), j...]
    unnamed x4 -> x2, local copies, waits for them, and re-layouts: 6.67 us -> 3.83 us
    reshape x2 -> x0, local copies, waits for them, and re-layouts: 1.79 us -> none  [body(): core.reshape(8, 2, 2, 2, 2, 8, 2, 64).transpose(7, 5, 4, 2, 0, 1, 3, 6)]
where the time goes in v5:
time: 148 us
  Pallas kernels  143 us (97%)
  local copies, waits for them, and re-layouts  3.83 us (3%)
    pallas_call x1, Pallas kernels, body(): pl.pallas_call(kernel, out_shape=(jax.ShapeDtypeStruct((64, 512), F32), j...  143 us
    unnamed x2, local copies, waits for them, and re-layouts  3.83 us

profile of v5, /device:TPU:1, one launch (start us, length us, event | category | flops | bytes accessed | tf_op | source)
XLA Modules:
  0.0 147.9 jit_solution(2620223793474761365)
XLA Ops:
  0.6 143.4 %hooi.1 = (f32[64,512]{1,0:T(8,128)}, f32[2048,128]{1,0:T(8,128)}) custom-call(f32[8,4096,128]{2,1,0:T(8,128)} %bitcast.6, f32[64,128]{1,0:T(8,128)} %bitcast.10, f32[32,64]{1,0:T(8,128)} %three_hbm.1, f32[32,64]{1,0:T(8,128)} %two_hbm.1, f32[64,512]{1,0:T(8,128)} %bitcast.8), custom_call_target="tpu_custom_call" | custom-call | tf_op jit(solution)/shard_map/hooi/pallas_call | solution.py:476
  144.1 1.6 %copy.9 = f32[512,64]{0,1:T(8,128)} copy(f32[512,64]{0,1:T(8,128)} %bitcast.9) | data formatting | bytes 262144
  145.6 2.3 %copy.10 = f32[64,8,4,64]{3,2,1,0:T(4,128)} copy(f32[64,8,4,64]{3,2,1,0:T(4,128)} %bitcast.7) | data formatting | bytes 1048576

commit v6 on v5

--- a/solution.py
+++ b/solution.py
@@ -11,6 +11,7 @@
 BF16 = jnp.bfloat16
 CHUNKS = 8
 LAG = 2
+EARLY = 6
 PLANE = tuple(range(1, 8))
 FIBERS = tuple(sorted(range(1, 16), key=lambda d: -(min(d // 4, 4 - d // 4) + min(d % 4, 4 - d % 4))))
 
@@ -137,7 +138,7 @@
     tensor, four_hbm, three_hbm, two_hbm, one_hbm, updated, collected,
     four, three, two, one, dealt, four_stack, one_stack, three_own_block, two_own_block,
     staged, outgoing, incoming, halfway, contracted, fibers, two_all, three_all, three_stack, wide_high, wide_low,
-    fibers_high, fibers_low, partial, scattered, shared, state, core_out, core_in,
+    fibers_high, fibers_low, order, crossed, partial, scattered, shared, state, core_out, core_in,
     load_sem, factor_sem, own_sem, z_send, z_recv, fib_own_sem, f_send, f_recv,
     two_send, two_recv, three_send, three_recv, rs_send, rs_recv, ar_send, ar_recv, ag_send, ag_recv, core_send, core_recv,
 ):
@@ -211,15 +212,16 @@
             z_all(chunk, half).wait_send()
 
     def f_rows(chunk, half, device):
-        return fibers.at[pl.ds((device * CHUNKS + chunk) * 4, 4), half]
+        return fibers.at[chunk, device, :, half]
 
     def f_copy(chunk, half, d):
         device, peer = fib_peer(d)
-        return remote(contracted.at[chunk, half, peer], f_rows(chunk, half, fib), f_send, f_recv, device)
-
-    def f_all():
-        block = fibers.at[pl.ds(0, 15 * CHUNKS * 4)]
-        return remote(block, block, f_send, f_recv, fib_peer(1)[0])
+        return remote(contracted.at[chunk, half, peer], f_rows(chunk, half, fib), f_send.at[chunk // EARLY], f_recv.at[chunk // EARLY], device)
+
+    def f_all(late):
+        chunks = pl.ds(EARLY, CHUNKS - EARLY) if late else pl.ds(0, EARLY)
+        block = fibers.at[chunks, pl.ds(0, 15)]
+        return remote(block, block, f_send.at[late], f_recv.at[late], fib_peer(1)[0])
 
     def f_own(chunk, half):
         return pltpu.make_async_copy(contracted.at[chunk, half, fib], f_rows(chunk, half, fib), fib_own_sem.at[chunk, half])
@@ -269,7 +271,11 @@
             wide_high[z] = high
             wide_low[z] = low
         fetch(3).wait()
-        one_stack[...] = halves(one[...])
+        natural = lax.broadcasted_iota(jnp.int32, (512, 512), 1)
+        there = ((natural >> 2) & 7) * 64 + (natural >> 5) * 4 + (natural & 3)
+        same = there == lax.broadcasted_iota(jnp.int32, (512, 512), 0)
+        order[...] = jnp.where(same, 1.0, 0.0).astype(BF16)
+        one_stack[...] = dot_nt(halves(one[...]), order[...]).astype(BF16)
 
     def modes_three_two(chunk, half):
         def rank(r):
@@ -345,21 +351,31 @@
     each(0, CHUNKS + LAG, advance)
     each(CHUNKS - 2, CHUNKS, sent_chunk)
     partial[...] = jnp.zeros_like(partial)
-    each(0, CHUNKS, lambda chunk: each(0, 2, lambda half: f_own(chunk, half).wait()))
-    f_all().wait_recv()
+    each(0, EARLY, lambda chunk: each(0, 2, lambda half: f_own(chunk, half).wait()))
+    f_all(0).wait_recv()
     fiber_rows = fibers.reshape(8192, 128)
 
-    def cross(step):
-        block = jnp.concatenate([fiber_rows[pl.ds(2 * step + n, 512, stride=16), :] for n in range(2)], axis=1)
-        high, low = split(block)
-        fibers_high[step] = high
-        fibers_low[step] = low
-        both = dot(one_stack[...], high)
-        both_parts = halves(both[:64] + both[64:] + dot(one_stack[:64, :], low))
-        back = dot_nt(both_parts, high)
-        partial[...] += back[:64] + back[64:] + dot_nt(both_parts[:64], low)
-
-    each(0, 8, cross, unroll=2)
+    def cross(step, first, count):
+        block = [fiber_rows[pl.ds(first * 16 + 2 * step + n, count, stride=16), :] for n in range(2)]
+        high, low = split(jnp.concatenate(block, axis=1))
+        fibers_high[step, pl.ds(first, count), :] = high
+        fibers_low[step, pl.ds(first, count), :] = low
+        both = dot(one_stack[:, first : first + count], high)
+        return both[:64] + both[64:] + dot(one_stack[:64, first : first + count], low)
+
+    def cross_early(step):
+        crossed[step] = cross(step, 0, EARLY * 64)
+
+    each(0, 8, cross_early, unroll=2)
+    each(EARLY, CHUNKS, lambda chunk: each(0, 2, lambda half: f_own(chunk, half).wait()))
+    f_all(1).wait_recv()
+
+    def cross_late(step):
+        parts = halves(crossed[step] + cross(step, EARLY * 64, (CHUNKS - EARLY) * 64))
+        back = dot_nt(parts, fibers_high[step])
+        partial[...] += back[:64] + back[64:] + dot_nt(parts[:64], fibers_low[step])
+
+    each(0, 8, cross_late, unroll=2)
 
     def rs_copy(d):
         device, peer = plane_peer(d)
@@ -411,21 +427,22 @@
                 at = pl.ds(pl.multiple_of(middle * 16 + high * 8, 8), 8)
                 core_out[peer, p_low, at, :] = across[start : start + 8, :]
 
-    each(0, 8, project, unroll=2)
-
-    def core_copy(d):
+    def core_copy(p_low, d):
         device, peer = plane_peer(d)
-        return remote(core_out.at[peer], core_in.at[:, me], core_send, core_recv, device)
-
-    def core_all():
-        block = core_in.at[:, pl.ds(0, 7)]
-        return remote(block, block, core_send, core_recv, plane_peer(1)[0])
-
-    for d in PLANE:
-        core_copy(d).start()
+        return remote(core_out.at[peer, p_low], core_in.at[p_low, me], core_send.at[p_low], core_recv.at[p_low], device)
+
+    def core_all(p_low):
+        block = core_in.at[p_low, pl.ds(0, 7)]
+        return remote(block, block, core_send.at[p_low], core_recv.at[p_low], plane_peer(1)[0])
+
+    def project_some(p_low):
+        each(p_low * 4, p_low * 4 + 4, project, unroll=2)
+        for d in PLANE:
+            core_copy(p_low, d).start()
+        core_in[p_low, me] = core_out[me, p_low]
+
     for p_low in range(2):
-        core_in[p_low, me] = core_out[me, p_low]
-
+        project_some(p_low)
     ag_all().wait_send()
     lanes = lax.broadcasted_iota(jnp.int32, (64, 128), 1)
     state[:, 512:] = jnp.where(lanes == lax.broadcasted_iota(jnp.int32, (64, 128), 0), 1.0, 0.0)
@@ -436,11 +453,17 @@
         state[...] = jnp.dot(eliminate(crossed), state[...], precision=HIGHEST, preferred_element_type=F32)
 
     each(0, 2, cholesky_qr)
-    updated[...] = state[:, :512]
+    rows = state[:, :512]
+    high = rows.astype(BF16)
+    rest = rows - high.astype(F32)
+    middle, low = split(rest)
+    moved = dot(jnp.concatenate([high, middle, low], axis=0), order[...])
+    updated[...] = moved[:64] + (moved[64:128] + moved[128:])
     inverse = state[:, 512:]
     weights = halves(jnp.concatenate([inverse, pltpu.roll(inverse, 64, 1)], axis=0))
 
-    core_all().wait_recv()
+    core_all(0).wait_recv()
+    core_all(1).wait_recv()
     core_rows = core_in.reshape(1024, 128)
 
     def finish(n):
@@ -461,12 +484,14 @@
 
     each(0, 4, finish)
 
-    core_all().wait_send()
+    core_all(0).wait_send()
+    core_all(1).wait_send()
     rs_all().wait_send()
     ar_all().wait_send()
     two_arrived().wait_send()
     three_copy().wait_send()
-    f_all().wait_send()
+    f_all(0).wait_send()
+    f_all(1).wait_send()
 
 
 def body(tensor, factor_one, factor_two, factor_three, factor_four):
@@ -493,7 +518,7 @@
             pltpu.VMEM((CHUNKS, 2, 1024, 128), F32),
             pltpu.VMEM((4, 256, 128), F32),
             pltpu.VMEM((CHUNKS, 2, 16, 4, 8, 128), F32),
-            pltpu.VMEM((512, 2, 8, 128), F32),
+            pltpu.VMEM((CHUNKS, 16, 4, 2, 8, 128), F32),
             pltpu.VMEM((4, 32, 128), F32),
             pltpu.VMEM((2, 64, 256), F32),
             pltpu.VMEM((64, 256), BF16),
@@ -501,14 +526,16 @@
             pltpu.VMEM((4, 128, 256), BF16),
             pltpu.VMEM((8, 512, 256), BF16),
             pltpu.VMEM((8, 512, 256), BF16),
+            pltpu.VMEM((512, 512), BF16),
+            pltpu.VMEM((8, 64, 256), F32),
             pltpu.VMEM((64, 512), F32),
             pltpu.VMEM((8, 8, 512), F32),
             pltpu.VMEM((16, 8, 512), F32),
             pltpu.VMEM((64, 640), F32),
             pltpu.VMEM((8, 2, 64, 128), F32),
             pltpu.VMEM((2, 8, 64, 128), F32),
-            dma((3,)), dma((4,)), dma((CHUNKS, 2)), dma((CHUNKS, 2)), dma((CHUNKS, 2)), dma((CHUNKS, 2)), dma(()), dma(()),
-            dma(()), dma(()), dma(()), dma(()), dma(()), dma(()), dma(()), dma(()), dma(()), dma(()), dma(()), dma(()),
+            dma((3,)), dma((4,)), dma((CHUNKS, 2)), dma((CHUNKS, 2)), dma((CHUNKS, 2)), dma((CHUNKS, 2)), dma((2,)), dma((2,)),
+            dma(()), dma(()), dma(()), dma(()), dma(()), dma(()), dma(()), dma(()), dma(()), dma(()), dma((2,)), dma((2,)),
         ],
         compiler_params=pltpu.CompilerParams(collective_id=0, has_side_effects=True, vmem_limit_bytes=56 * 2**20),
         name="hooi",

time: 148 us -> 146 us (0.986)
  Pallas kernels: 143 us -> 141 us
    pallas_call x1, Pallas kernels: 143 us -> 141 us  [body(): pl.pallas_call(kernel, out_shape=(jax.ShapeDtypeStruct((64, 512), F32), j...]
where the time goes in v6:
time: 146 us
  Pallas kernels  141 us (97%)
  local copies, waits for them, and re-layouts  3.83 us (3%)
    pallas_call x1, Pallas kernels, body(): pl.pallas_call(kernel, out_shape=(jax.ShapeDtypeStruct((64, 512), F32), j...  141 us
    unnamed x2, local copies, waits for them, and re-layouts  3.83 us

profile of v6, /device:TPU:1, one launch (start us, length us, event | category | flops | bytes accessed | tf_op | source)
XLA Modules:
  0.0 145.6 jit_solution(15430698840510332120)
XLA Ops:
  0.6 141.1 %hooi.1 = (f32[64,512]{1,0:T(8,128)}, f32[2048,128]{1,0:T(8,128)}) custom-call(f32[8,4096,128]{2,1,0:T(8,128)} %bitcast.6, f32[64,128]{1,0:T(8,128)} %bitcast.10, f32[32,64]{1,0:T(8,128)} %three_hbm.1, f32[32,64]{1,0:T(8,128)} %two_hbm.1, f32[64,512]{1,0:T(8,128)} %bitcast.8), custom_call_target="tpu_custom_call" | custom-call | tf_op jit(solution)/shard_map/hooi/pallas_call | solution.py:501
  141.7 1.6 %copy.9 = f32[512,64]{0,1:T(8,128)} copy(f32[512,64]{0,1:T(8,128)} %bitcast.9) | data formatting | bytes 262144
  143.3 2.3 %copy.10 = f32[64,8,4,64]{3,2,1,0:T(4,128)} copy(f32[64,8,4,64]{3,2,1,0:T(4,128)} %bitcast.7) | data formatting | bytes 1048576

commit v7 on v6

--- a/solution.py
+++ b/solution.py
@@ -11,7 +11,7 @@
 BF16 = jnp.bfloat16
 CHUNKS = 8
 LAG = 2
-EARLY = 6
+EARLY = 7
 PLANE = tuple(range(1, 8))
 FIBERS = tuple(sorted(range(1, 16), key=lambda d: -(min(d // 4, 4 - d // 4) + min(d % 4, 4 - d % 4))))
 
@@ -135,12 +135,12 @@
 
 
 def kernel(
-    tensor, four_hbm, three_hbm, two_hbm, one_hbm, updated, collected,
+    tensor, four_hbm, three_hbm, two_hbm, one_hbm, updated, inverse, received,
     four, three, two, one, dealt, four_stack, one_stack, three_own_block, two_own_block,
     staged, outgoing, incoming, halfway, contracted, fibers, two_all, three_all, three_stack, wide_high, wide_low,
     fibers_high, fibers_low, order, crossed, partial, scattered, shared, state, core_out, core_in,
     load_sem, factor_sem, own_sem, z_send, z_recv, fib_own_sem, f_send, f_recv,
-    two_send, two_recv, three_send, three_recv, rs_send, rs_recv, ar_send, ar_recv, ag_send, ag_recv, core_send, core_recv,
+    two_send, two_recv, three_send, three_recv, rs_send, rs_recv, ar_send, ar_recv, ag_send, ag_recv, core_send, core_recv, out_sem,
 ):
     fib, row, slab = place()
     me = row * 2 + slab
@@ -459,30 +459,11 @@
     middle, low = split(rest)
     moved = dot(jnp.concatenate([high, middle, low], axis=0), order[...])
     updated[...] = moved[:64] + (moved[64:128] + moved[128:])
-    inverse = state[:, 512:]
-    weights = halves(jnp.concatenate([inverse, pltpu.roll(inverse, 64, 1)], axis=0))
-
-    core_all(0).wait_recv()
-    core_all(1).wait_recv()
-    core_rows = core_in.reshape(1024, 128)
-
-    def finish(n):
-        start = (n % 2) * 512 + (n // 2) * 8
-        block = jnp.concatenate([core_rows[pl.ds(start + q, 32, stride=16), :] for q in range(8)], axis=0)
-        high, low = split(block)
-        both = dot_nt(weights, high)
-        out = both[:128] + both[128:] + dot_nt(weights[:128], low)
-        for q in range(8):
-            tile, off = q // 4, (q % 4) * 32
-            lower = out[:64, tile * 128 : tile * 128 + 128]
-            upper = out[64:, tile * 128 : tile * 128 + 128]
-            if off:
-                lower = pltpu.roll(lower, 128 - off, 1)
-            if off != 32:
-                upper = pltpu.roll(upper, (160 - off) % 128, 1)
-            collected[pl.ds(q * 4 + n, 64, stride=32), :] = jnp.where(lanes < 32, lower, upper)
-
-    each(0, 4, finish)
+    inverse[...] = state[:, 512:]
+    for p_low in range(2):
+        core_all(p_low).wait_recv()
+    out_copy = pltpu.make_async_copy(core_in, received, out_sem)
+    out_copy.start()
 
     core_all(0).wait_send()
     core_all(1).wait_send()
@@ -492,17 +473,51 @@
     three_copy().wait_send()
     f_all(0).wait_send()
     f_all(1).wait_send()
+    out_copy.wait()
+
+
+def finish_kernel(received, inverse, rows, updated, core, high, low):
+    step = pl.program_id(0)
+
+    @pl.when(step == 0)
+    def _():
+        updated[...] = rows[...]
+        flat = received.reshape(1024, 128)
+        for n in range(32):
+            p, q = n // 8, n % 8
+            part = flat[pl.ds((p % 2) * 512 + (p // 2) * 8 + q, 32, stride=16), :]
+            high[pl.ds(n * 32, 32), :], low[pl.ds(n * 32, 32), :] = split(part)
+
+    own = inverse[pl.ds(pl.multiple_of(step * 16, 16), 16), :]
+    weights = halves(jnp.concatenate([own, pltpu.roll(own, 64, 1)], axis=0))
+    both = dot_nt(weights, high[...])
+    out = both[:32] + both[32:] + dot_nt(weights[:32], low[...])
+    lanes = lax.broadcasted_iota(jnp.int32, (16, 128), 1)
+    for n in range(32):
+        p, q = n // 8, n % 8
+        tile, off = n // 4, (n % 4) * 32
+        lower = out[:16, tile * 128 : tile * 128 + 128]
+        upper = out[16:, tile * 128 : tile * 128 + 128]
+        if off:
+            lower = pltpu.roll(lower, 128 - off, 1)
+        if off != 32:
+            upper = pltpu.roll(upper, (160 - off) % 128, 1)
+        core[pl.ds(q * 4 + p, 16, stride=32), :] = jnp.where(lanes < 32, lower, upper)
 
 
 def body(tensor, factor_one, factor_two, factor_three, factor_four):
     vmem = pl.BlockSpec(memory_space=pltpu.VMEM)
     hbm = pl.BlockSpec(memory_space=pl.ANY)
     dma = pltpu.SemaphoreType.DMA
-    updated, core = pl.pallas_call(
+    rows, inverse, received = pl.pallas_call(
         kernel,
-        out_shape=(jax.ShapeDtypeStruct((64, 512), F32), jax.ShapeDtypeStruct((2048, 128), F32)),
+        out_shape=(
+            jax.ShapeDtypeStruct((64, 512), F32),
+            jax.ShapeDtypeStruct((64, 128), F32),
+            jax.ShapeDtypeStruct((2, 8, 64, 128), F32),
+        ),
         in_specs=[hbm] * 5,
-        out_specs=(vmem, vmem),
+        out_specs=(vmem, vmem, hbm),
         scratch_shapes=[
             pltpu.VMEM((64, 128), F32),
             pltpu.VMEM((32, 64), F32),
@@ -535,11 +550,22 @@
             pltpu.VMEM((8, 2, 64, 128), F32),
             pltpu.VMEM((2, 8, 64, 128), F32),
             dma((3,)), dma((4,)), dma((CHUNKS, 2)), dma((CHUNKS, 2)), dma((CHUNKS, 2)), dma((CHUNKS, 2)), dma((2,)), dma((2,)),
-            dma(()), dma(()), dma(()), dma(()), dma(()), dma(()), dma(()), dma(()), dma(()), dma(()), dma((2,)), dma((2,)),
+            dma(()), dma(()), dma(()), dma(()), dma(()), dma(()), dma(()), dma(()), dma(()), dma(()), dma((2,)), dma((2,)), dma(()),
         ],
         compiler_params=pltpu.CompilerParams(collective_id=0, has_side_effects=True, vmem_limit_bytes=56 * 2**20),
         name="hooi",
     )(tensor.reshape(8, 4096, 128), factor_four.T, factor_three, factor_two, factor_one.T)
+    whole = lambda *shape: pl.BlockSpec(shape, lambda step: (0,) * len(shape))
+    updated, core = pl.pallas_call(
+        finish_kernel,
+        grid=(4,),
+        out_shape=(jax.ShapeDtypeStruct((64, 512), F32), jax.ShapeDtypeStruct((2048, 128), F32)),
+        in_specs=[whole(2, 8, 64, 128), whole(64, 128), whole(64, 512)],
+        out_specs=(whole(64, 512), pl.BlockSpec((512, 128), lambda step: (step, 0))),
+        scratch_shapes=[pltpu.VMEM((1024, 128), BF16), pltpu.VMEM((1024, 128), BF16)],
+        compiler_params=pltpu.CompilerParams(vmem_limit_bytes=62 * 2**20),
+        name="finish",
+    )(received, inverse, rows)
     return (updated.T, core[:, :64].reshape(64, 8, 4, 64))
 
 

time: 146 us -> 145 us (level)
  local copies, waits for them, and re-layouts: 3.83 us -> 0 us
  Pallas kernels: 141 us -> 144 us
    pallas_call x0 -> x1, Pallas kernels: none -> 4.15 us  [body(): pl.pallas_call(finish_kernel, grid=(4,), out_shape=(jax.ShapeDtypeStruct(...]
    unnamed x2 -> x0, local copies, waits for them, and re-layouts: 3.83 us -> none
    pallas_call x1, Pallas kernels: 141 us -> 140 us  [body(): pl.pallas_call(kernel, out_shape=(jax.ShapeDtypeStruct((64, 512), F32), j...]
where the time goes in v7:
time: 145 us; the launch traced here: 144 us
  Pallas kernels  144 us (99%)
    pallas_call x1, Pallas kernels, body(): pl.pallas_call(kernel, out_shape=(jax.ShapeDtypeStruct((64, 512), F32), j...  140 us
    pallas_call x1, Pallas kernels, body(): pl.pallas_call(finish_kernel, grid=(4,), out_shape=(jax.ShapeDtypeStruct(...  4.15 us

profile of v7, /device:TPU:1, one launch (start us, length us, event | category | flops | bytes accessed | tf_op | source)
XLA Modules:
  0.0 144.4 jit_solution(6271334433717846929)
XLA Ops:
  0.6 139.6 %hooi.1 = (f32[64,512]{1,0:T(8,128)}, f32[64,128]{1,0:T(8,128)}, f32[2,8,64,128]{3,2,1,0:T(8,128)}) custom-call(f32[8,4096,128]{2,1,0:T(8,128)} %bitcast.6, f32[64,128]{1,0:T(8,128)} %bitcast.8, f32[32,64]{1,0:T(8,128)} %three_hbm.1, f32[32,64]{1,0:T(8,128)} %two_hbm.1, f32[64,512]{1,0:T(8,128)} %bitcast.7), custom_call_target="tpu_custom_call" | custom-call | tf_op jit(solution)/shard_map/hooi/pallas_call | solution.py:512
  140.3 4.1 %finish.1 = (f32[64,512]{1,0:T(8,128)}, f32[2048,128]{1,0:T(8,128)}) custom-call(f32[2,8,64,128]{3,2,1,0:T(8,128)} %get-tuple-element.7.received, f32[64,128]{1,0:T(8,128)} %get-tuple-element.8.inverse, f32[64,512]{1,0:T(8,128)} %get-tuple-element.9.rows), custom_call_target="tpu_custom_call" | custom-call | tf_op jit(solution)/shard_map/finish/pallas_call | solution.py:559

commit v8 on v7

--- a/solution.py
+++ b/solution.py
@@ -11,7 +11,7 @@
 BF16 = jnp.bfloat16
 CHUNKS = 8
 LAG = 2
-EARLY = 7
+EARLY = CHUNKS - 1
 PLANE = tuple(range(1, 8))
 FIBERS = tuple(sorted(range(1, 16), key=lambda d: -(min(d // 4, 4 - d // 4) + min(d % 4, 4 - d % 4))))
 
@@ -80,7 +80,7 @@
     return jnp.concatenate(split(x), axis=0)
 
 
-def eliminate(crossed, group=4):
+def eliminate(crossed, group=8):
     lane = lax.broadcasted_iota(jnp.int32, (8, 64), 1)
     row = lax.broadcasted_iota(jnp.int32, (8, 64), 0)
     below = lax.broadcasted_iota(jnp.int32, (8, 128), 0)
@@ -216,12 +216,12 @@
 
     def f_copy(chunk, half, d):
         device, peer = fib_peer(d)
-        return remote(contracted.at[chunk, half, peer], f_rows(chunk, half, fib), f_send.at[chunk // EARLY], f_recv.at[chunk // EARLY], device)
-
-    def f_all(late):
-        chunks = pl.ds(EARLY, CHUNKS - EARLY) if late else pl.ds(0, EARLY)
-        block = fibers.at[chunks, pl.ds(0, 15)]
-        return remote(block, block, f_send.at[late], f_recv.at[late], fib_peer(1)[0])
+        stage = (chunk // EARLY) * (1 + half)
+        return remote(contracted.at[chunk, half, peer], f_rows(chunk, half, fib), f_send.at[stage], f_recv.at[stage], device)
+
+    def f_all(stage):
+        block = fibers.at[pl.ds(0, EARLY), pl.ds(0, 15)] if stage == 0 else fibers.at[EARLY, pl.ds(0, 15), :, stage - 1]
+        return remote(block, block, f_send.at[stage], f_recv.at[stage], fib_peer(1)[0])
 
     def f_own(chunk, half):
         return pltpu.make_async_copy(contracted.at[chunk, half, fib], f_rows(chunk, half, fib), fib_own_sem.at[chunk, half])
@@ -288,7 +288,7 @@
             for z in range(4):
                 halfway[z, pl.ds(r, 64, stride=4), :] = out[:, z * 128 : (z + 1) * 128]
 
-        each(0, 4, rank, unroll=2)
+        each(0, 4, rank, unroll=4)
 
         def rows(block):
             at = pl.ds(pl.multiple_of(block * 128, 128), 128)
@@ -305,7 +305,7 @@
                     contracted[chunk, half, block * 8 + f, 2 * t] = jnp.where(left, lower, pltpu.roll(upper, 64, 1))
                     contracted[chunk, half, block * 8 + f, 2 * t + 1] = jnp.where(left, pltpu.roll(lower, 64, 1), upper)
 
-        each(0, 2, rows)
+        each(0, 2, rows, unroll=2)
 
     def advance(turn):
         @pl.when(turn < CHUNKS)
@@ -367,15 +367,16 @@
         crossed[step] = cross(step, 0, EARLY * 64)
 
     each(0, 8, cross_early, unroll=2)
-    each(EARLY, CHUNKS, lambda chunk: each(0, 2, lambda half: f_own(chunk, half).wait()))
-    f_all(1).wait_recv()
 
     def cross_late(step):
         parts = halves(crossed[step] + cross(step, EARLY * 64, (CHUNKS - EARLY) * 64))
         back = dot_nt(parts, fibers_high[step])
         partial[...] += back[:64] + back[64:] + dot_nt(parts[:64], fibers_low[step])
 
-    each(0, 8, cross_late, unroll=2)
+    for half in range(2):
+        f_own(EARLY, half).wait()
+        f_all(1 + half).wait_recv()
+        each(half * 4, half * 4 + 4, cross_late, unroll=4)
 
     def rs_copy(d):
         device, peer = plane_peer(d)
@@ -436,7 +437,7 @@
         return remote(block, block, core_send.at[p_low], core_recv.at[p_low], plane_peer(1)[0])
 
     def project_some(p_low):
-        each(p_low * 4, p_low * 4 + 4, project, unroll=2)
+        each(p_low * 4, p_low * 4 + 4, project, unroll=4)
         for d in PLANE:
             core_copy(p_low, d).start()
         core_in[p_low, me] = core_out[me, p_low]
@@ -473,6 +474,7 @@
     three_copy().wait_send()
     f_all(0).wait_send()
     f_all(1).wait_send()
+    f_all(2).wait_send()
     out_copy.wait()
 
 
@@ -488,21 +490,21 @@
             part = flat[pl.ds((p % 2) * 512 + (p // 2) * 8 + q, 32, stride=16), :]
             high[pl.ds(n * 32, 32), :], low[pl.ds(n * 32, 32), :] = split(part)
 
-    own = inverse[pl.ds(pl.multiple_of(step * 16, 16), 16), :]
+    own = inverse[pl.ds(pl.multiple_of(step * 32, 32), 32), :]
     weights = halves(jnp.concatenate([own, pltpu.roll(own, 64, 1)], axis=0))
     both = dot_nt(weights, high[...])
-    out = both[:32] + both[32:] + dot_nt(weights[:32], low[...])
-    lanes = lax.broadcasted_iota(jnp.int32, (16, 128), 1)
+    out = both[:64] + both[64:] + dot_nt(weights[:64], low[...])
+    lanes = lax.broadcasted_iota(jnp.int32, (32, 128), 1)
     for n in range(32):
         p, q = n // 8, n % 8
         tile, off = n // 4, (n % 4) * 32
-        lower = out[:16, tile * 128 : tile * 128 + 128]
-        upper = out[16:, tile * 128 : tile * 128 + 128]
+        lower = out[:32, tile * 128 : tile * 128 + 128]
+        upper = out[32:, tile * 128 : tile * 128 + 128]
         if off:
             lower = pltpu.roll(lower, 128 - off, 1)
         if off != 32:
             upper = pltpu.roll(upper, (160 - off) % 128, 1)
-        core[pl.ds(q * 4 + p, 16, stride=32), :] = jnp.where(lanes < 32, lower, upper)
+        core[pl.ds(q * 4 + p, 32, stride=32), :] = jnp.where(lanes < 32, lower, upper)
 
 
 def body(tensor, factor_one, factor_two, factor_three, factor_four):
@@ -549,7 +551,7 @@
             pltpu.VMEM((64, 640), F32),
             pltpu.VMEM((8, 2, 64, 128), F32),
             pltpu.VMEM((2, 8, 64, 128), F32),
-            dma((3,)), dma((4,)), dma((CHUNKS, 2)), dma((CHUNKS, 2)), dma((CHUNKS, 2)), dma((CHUNKS, 2)), dma((2,)), dma((2,)),
+            dma((3,)), dma((4,)), dma((CHUNKS, 2)), dma((CHUNKS, 2)), dma((CHUNKS, 2)), dma((CHUNKS, 2)), dma((3,)), dma((3,)),
             dma(()), dma(()), dma(()), dma(()), dma(()), dma(()), dma(()), dma(()), dma(()), dma(()), dma((2,)), dma((2,)), dma(()),
         ],
         compiler_params=pltpu.CompilerParams(collective_id=0, has_side_effects=True, vmem_limit_bytes=56 * 2**20),
@@ -558,10 +560,10 @@
     whole = lambda *shape: pl.BlockSpec(shape, lambda step: (0,) * len(shape))
     updated, core = pl.pallas_call(
         finish_kernel,
-        grid=(4,),
+        grid=(2,),
         out_shape=(jax.ShapeDtypeStruct((64, 512), F32), jax.ShapeDtypeStruct((2048, 128), F32)),
         in_specs=[whole(2, 8, 64, 128), whole(64, 128), whole(64, 512)],
-        out_specs=(whole(64, 512), pl.BlockSpec((512, 128), lambda step: (step, 0))),
+        out_specs=(whole(64, 512), pl.BlockSpec((1024, 128), lambda step: (step, 0))),
         scratch_shapes=[pltpu.VMEM((1024, 128), BF16), pltpu.VMEM((1024, 128), BF16)],
         compiler_params=pltpu.CompilerParams(vmem_limit_bytes=62 * 2**20),
         name="finish",

time: 145 us -> 142 us (0.979)
  Pallas kernels: 144 us -> 141 us
    pallas_call x1, Pallas kernels: 140 us -> 137 us  [body(): pl.pallas_call(kernel, out_shape=(jax.ShapeDtypeStruct((64, 512), F32), j...]
where the time goes in v8:
time: 142 us
  Pallas kernels  141 us (99%)
    pallas_call x1, Pallas kernels, body(): pl.pallas_call(kernel, out_shape=(jax.ShapeDtypeStruct((64, 512), F32), j...  137 us
    pallas_call x1, Pallas kernels, body(): pl.pallas_call(finish_kernel, grid=(2,), out_shape=(jax.ShapeDtypeStruct(...  3.66 us

profile of v8, /device:TPU:1, one launch (start us, length us, event | category | flops | bytes accessed | tf_op | source)
XLA Modules:
  0.0 141.7 jit_solution(12796002030873876939)
XLA Ops:
  0.6 137.4 %hooi.1 = (f32[64,512]{1,0:T(8,128)}, f32[64,128]{1,0:T(8,128)}, f32[2,8,64,128]{3,2,1,0:T(8,128)}) custom-call(f32[8,4096,128]{2,1,0:T(8,128)} %bitcast.6, f32[64,128]{1,0:T(8,128)} %bitcast.8, f32[32,64]{1,0:T(8,128)} %three_hbm.1, f32[32,64]{1,0:T(8,128)} %two_hbm.1, f32[64,512]{1,0:T(8,128)} %bitcast.7), custom_call_target="tpu_custom_call" | custom-call | tf_op jit(solution)/shard_map/hooi/pallas_call | solution.py:514
  138.1 3.7 %finish.1 = (f32[64,512]{1,0:T(8,128)}, f32[2048,128]{1,0:T(8,128)}) custom-call(f32[2,8,64,128]{3,2,1,0:T(8,128)} %get-tuple-element.7.received, f32[64,128]{1,0:T(8,128)} %get-tuple-element.8.inverse, f32[64,512]{1,0:T(8,128)} %get-tuple-element.9.rows), custom_call_target="tpu_custom_call" | custom-call | tf_op jit(solution)/shard_map/finish/pallas_call | solution.py:561

commit v9 on v8

--- a/solution.py
+++ b/solution.py
@@ -12,7 +12,7 @@
 CHUNKS = 8
 LAG = 2
 EARLY = CHUNKS - 1
-PLANE = tuple(range(1, 8))
+PLANE = (4, 2, 6, 5, 3, 7, 1)
 FIBERS = tuple(sorted(range(1, 16), key=lambda d: -(min(d // 4, 4 - d // 4) + min(d % 4, 4 - d % 4))))
 
 
@@ -428,22 +428,22 @@
                 at = pl.ds(pl.multiple_of(middle * 16 + high * 8, 8), 8)
                 core_out[peer, p_low, at, :] = across[start : start + 8, :]
 
-    def core_copy(p_low, d):
+    def core_copy(p_low, pair, d):
         device, peer = plane_peer(d)
-        return remote(core_out.at[peer, p_low], core_in.at[p_low, me], core_send.at[p_low], core_recv.at[p_low], device)
+        rows = pl.ds(pair * 32, 32)
+        return remote(core_out.at[peer, p_low, rows, :], core_in.at[p_low, me, rows, :], core_send.at[p_low], core_recv.at[p_low], device)
 
     def core_all(p_low):
         block = core_in.at[p_low, pl.ds(0, 7)]
         return remote(block, block, core_send.at[p_low], core_recv.at[p_low], plane_peer(1)[0])
 
-    def project_some(p_low):
-        each(p_low * 4, p_low * 4 + 4, project, unroll=4)
-        for d in PLANE:
-            core_copy(p_low, d).start()
+    for p_low in range(2):
+        for pair in range(2):
+            first = p_low * 4 + pair * 2
+            each(first, first + 2, project, unroll=2)
+            for d in PLANE:
+                core_copy(p_low, pair, d).start()
         core_in[p_low, me] = core_out[me, p_low]
-
-    for p_low in range(2):
-        project_some(p_low)
     ag_all().wait_send()
     lanes = lax.broadcasted_iota(jnp.int32, (64, 128), 1)
     state[:, 512:] = jnp.where(lanes == lax.broadcasted_iota(jnp.int32, (64, 128), 0), 1.0, 0.0)
@@ -461,10 +461,13 @@
     moved = dot(jnp.concatenate([high, middle, low], axis=0), order[...])
     updated[...] = moved[:64] + (moved[64:128] + moved[128:])
     inverse[...] = state[:, 512:]
+
+    def out_copy(p_low):
+        return pltpu.make_async_copy(core_in.at[p_low], received.at[p_low], out_sem.at[p_low])
+
     for p_low in range(2):
         core_all(p_low).wait_recv()
-    out_copy = pltpu.make_async_copy(core_in, received, out_sem)
-    out_copy.start()
+        out_copy(p_low).start()
 
     core_all(0).wait_send()
     core_all(1).wait_send()
@@ -475,7 +478,8 @@
     f_all(0).wait_send()
     f_all(1).wait_send()
     f_all(2).wait_send()
-    out_copy.wait()
+    out_copy(0).wait()
+    out_copy(1).wait()
 
 
 def finish_kernel(received, inverse, rows, updated, core, high, low):
@@ -552,7 +556,7 @@
             pltpu.VMEM((8, 2, 64, 128), F32),
             pltpu.VMEM((2, 8, 64, 128), F32),
             dma((3,)), dma((4,)), dma((CHUNKS, 2)), dma((CHUNKS, 2)), dma((CHUNKS, 2)), dma((CHUNKS, 2)), dma((3,)), dma((3,)),
-            dma(()), dma(()), dma(()), dma(()), dma(()), dma(()), dma(()), dma(()), dma(()), dma(()), dma((2,)), dma((2,)), dma(()),
+            dma(()), dma(()), dma(()), dma(()), dma(()), dma(()), dma(()), dma(()), dma(()), dma(()), dma((2,)), dma((2,)), dma((2,)),
         ],
         compiler_params=pltpu.CompilerParams(collective_id=0, has_side_effects=True, vmem_limit_bytes=56 * 2**20),
         name="hooi",

time: 142 us -> 140 us (0.986)
    pallas_call x1, Pallas kernels: 137 us -> 136 us  [body(): pl.pallas_call(kernel, out_shape=(jax.ShapeDtypeStruct((64, 512), F32), j...]
where the time goes in v9:
time: 140 us
  Pallas kernels  140 us (100%)
    pallas_call x1, Pallas kernels, body(): pl.pallas_call(kernel, out_shape=(jax.ShapeDtypeStruct((64, 512), F32), j...  136 us
    pallas_call x1, Pallas kernels, body(): pl.pallas_call(finish_kernel, grid=(2,), out_shape=(jax.ShapeDtypeStruct(...  3.66 us

profile of v9, /device:TPU:1, one launch (start us, length us, event | category | flops | bytes accessed | tf_op | source)
XLA Modules:
  0.0 140.3 jit_solution(907945100969814715)
XLA Ops:
  0.6 136.0 %hooi.1 = (f32[64,512]{1,0:T(8,128)}, f32[64,128]{1,0:T(8,128)}, f32[2,8,64,128]{3,2,1,0:T(8,128)}) custom-call(f32[8,4096,128]{2,1,0:T(8,128)} %bitcast.6, f32[64,128]{1,0:T(8,128)} %bitcast.8, f32[32,64]{1,0:T(8,128)} %three_hbm.1, f32[32,64]{1,0:T(8,128)} %two_hbm.1, f32[64,512]{1,0:T(8,128)} %bitcast.7), custom_call_target="tpu_custom_call" | custom-call | tf_op jit(solution)/shard_map/hooi/pallas_call | solution.py:518
  136.6 3.7 %finish.1 = (f32[64,512]{1,0:T(8,128)}, f32[2048,128]{1,0:T(8,128)}) custom-call(f32[2,8,64,128]{3,2,1,0:T(8,128)} %get-tuple-element.7.received, f32[64,128]{1,0:T(8,128)} %get-tuple-element.8.inverse, f32[64,512]{1,0:T(8,128)} %get-tuple-element.9.rows), custom_call_target="tpu_custom_call" | custom-call | tf_op jit(solution)/shard_map/finish/pallas_call | solution.py:565

commit v10 on v9

--- a/solution.py
+++ b/solution.py
@@ -160,7 +160,7 @@
             outgoing[chunk, pl.ds(2 * pair, 64, stride=32), :] = out[:, :128]
             outgoing[chunk, pl.ds(2 * pair + 1, 64, stride=32), :] = out[:, 128:]
 
-        each(0, 16, two_steps, unroll=2)
+        each(0, 16, two_steps, unroll=4)
 
     def fetch(n):
         source, target = ((four_hbm, four), (three_hbm, three), (two_hbm, two), (one_hbm, one))[n]

time: 140 us -> 140 us (level)
  no operation moved by 1% of the time
where the time goes in v10:
time: 140 us; the launch traced here: 139 us
  Pallas kernels  139 us (99%)
    pallas_call x1, Pallas kernels, body(): pl.pallas_call(kernel, out_shape=(jax.ShapeDtypeStruct((64, 512), F32), j...  135 us
    pallas_call x1, Pallas kernels, body(): pl.pallas_call(finish_kernel, grid=(2,), out_shape=(jax.ShapeDtypeStruct(...  3.67 us

profile of v10, /device:TPU:1, one launch (start us, length us, event | category | flops | bytes accessed | tf_op | source)
XLA Modules:
  0.0 139.4 jit_solution(3062942805707847784)
XLA Ops:
  0.6 135.1 %hooi.1 = (f32[64,512]{1,0:T(8,128)}, f32[64,128]{1,0:T(8,128)}, f32[2,8,64,128]{3,2,1,0:T(8,128)}) custom-call(f32[8,4096,128]{2,1,0:T(8,128)} %bitcast.6, f32[64,128]{1,0:T(8,128)} %bitcast.8, f32[32,64]{1,0:T(8,128)} %three_hbm.1, f32[32,64]{1,0:T(8,128)} %two_hbm.1, f32[64,512]{1,0:T(8,128)} %bitcast.7), custom_call_target="tpu_custom_call" | custom-call | tf_op jit(solution)/shard_map/hooi/pallas_call | solution.py:518
  135.8 3.7 %finish.1 = (f32[64,512]{1,0:T(8,128)}, f32[2048,128]{1,0:T(8,128)}) custom-call(f32[2,8,64,128]{3,2,1,0:T(8,128)} %get-tuple-element.7.received, f32[64,128]{1,0:T(8,128)} %get-tuple-element.8.inverse, f32[64,512]{1,0:T(8,128)} %get-tuple-element.9.rows), custom_call_target="tpu_custom_call" | custom-call | tf_op jit(solution)/shard_map/finish/pallas_call | solution.py:565
